TPU v7x, 32 devices: a whole 2x2x4 slice. The times are simulated.
32 devices in a mesh: row: 4 (over x, core), col: 2 (over y), pair: 4 (over z).
Axes of the slice: x: 2, y: 2, z: 4, core: 2. Of those that a mesh axis runs over, the one named last changes fastest.
Arguments:
- frames: bfloat16 [4, 2, 64, 64, 256], P('pair', None, 'row', 'col'), may hold values from -6 to 6
- offsets: int32 [4, 2, 2, 2], P('pair'), may hold values from -8 to 8, as said below
- weight: bfloat16 [3, 3, 256, 256], replicated, may hold values from -0.125 to 0.125
- bias: float32 [256], replicated, may hold values from -3 to 3
- cotangent: bfloat16 [4, 81, 64, 64], P('pair', None, 'row', 'col'), may hold values from -0.023925781 to 0.023925781
Outputs:
- corr: bfloat16 [4, 81, 64, 64], P('pair', None, 'row', 'col')
- grad_weight: float32 [3, 3, 256, 256], replicated
- grad_bias: float32 [256], replicated
Inputs may be any that keep to these rules, and one draw needn't show every extreme that they name: `offsets`: entry [.., 0] shifts rows and [.., 1] columns of one 32 x 32 block; both ends of the range occur in every draw.
All inputs are finite; a program needn't handle non-finite values.
Results may differ from a plain program's by a relative error of at most 0.0046.
Values may be sent and summed in bfloat16 or wider, within the bound.
A program may use at most 64 MiB of HBM per device.

v0:
```python
import jax
import jax.numpy as jnp
from jax import lax
from jax.sharding import PartitionSpec as P

BLK = 32
RAD = 4
MAXOFF = 8


def with_halo(cells, sides, width):
    for axis, dim in sides:
        count = lax.axis_size(axis)
        ends = count - 1
        head = lax.slice_in_dim(cells, 0, width, axis=dim)
        tail = lax.slice_in_dim(cells, cells.shape[dim] - width, cells.shape[dim], axis=dim)
        cells = jnp.concatenate(
            [
                lax.ppermute(tail, axis, [(i, (i + 1) % count) for i in range(ends)]),
                cells,
                lax.ppermute(head, axis, [((i + 1) % count, i) for i in range(ends)]),
            ],
            axis=dim,
        )
    return cells


def band_take(scores):
    row_count, col_count, patch_width = scores.shape
    widened = jnp.pad(scores, ((0, 0), (0, 0), (0, 1)))
    flattened = widened.reshape(row_count, col_count * (patch_width + 1))
    flattened = jnp.pad(flattened, ((0, 0), (0, col_count)))
    return flattened.reshape(row_count, col_count, patch_width + 2)[:, :, : 2 * RAD + 1]


def band_spread(bands, patch_width):
    row_count, col_count, window_size = bands.shape
    widened = jnp.pad(bands, ((0, 0), (0, 0), (0, patch_width + 2 - window_size)))
    flattened = widened.reshape(row_count, col_count * (patch_width + 2))[
        :, : col_count * (patch_width + 1)
    ]
    return flattened.reshape(row_count, col_count, patch_width + 1)[:, :, :patch_width]


def block_scores(block_one, window_two):
    row_count, col_count = (block_one.shape[0], block_one.shape[1])
    window_size = 2 * RAD + 1
    score_list = []
    for row_shift in range(window_size):
        scores = jnp.einsum(
            "yxc,yzc->yxz",
            block_one,
            window_two[row_shift : row_shift + row_count],
            preferred_element_type=jnp.float32,
        )
        score_list.append(band_take(scores))
    stacked = jnp.stack(score_list)
    return jnp.transpose(stacked, (0, 3, 1, 2)).reshape(
        window_size * window_size, row_count, col_count
    )


def block_grads(cot_block, block_one, window_two):
    row_count, col_count, channels = block_one.shape
    window_size = 2 * RAD + 1
    patch_width = col_count + 2 * RAD
    cot_grid = jnp.transpose(
        cot_block.reshape(window_size, window_size, row_count, col_count), (0, 2, 3, 1)
    )
    grad_block = jnp.zeros((row_count, col_count, channels), jnp.float32)
    grad_window = jnp.zeros((row_count + 2 * RAD, patch_width, channels), jnp.float32)
    for row_shift in range(window_size):
        spread = band_spread(cot_grid[row_shift], patch_width)
        grad_block = grad_block + jnp.einsum(
            "yxz,yzc->yxc",
            spread,
            window_two[row_shift : row_shift + row_count],
            preferred_element_type=jnp.float32,
        )
        patch_term = jnp.einsum(
            "yxz,yxc->yzc", spread, block_one, preferred_element_type=jnp.float32
        )
        grad_window = grad_window.at[row_shift : row_shift + row_count].add(patch_term)
    return (grad_block, grad_window)


def convolve(padded, weight, bias, row_count, col_count):
    channels = weight.shape[3]
    accumulated = jnp.zeros((row_count * col_count, channels), jnp.float32)
    for tap_row in range(3):
        for tap_col in range(3):
            window = padded[tap_row : tap_row + row_count, tap_col : tap_col + col_count].reshape(
                row_count * col_count, -1
            )
            accumulated = accumulated + jnp.dot(
                window, weight[tap_row, tap_col], preferred_element_type=jnp.float32
            )
    return accumulated.reshape(row_count, col_count, channels) + bias


def weight_terms(padded, delta, input_float):
    row_count, col_count, channels = delta.shape
    flat_delta = delta.reshape(row_count * col_count, channels)
    tap_list = []
    for tap_row in range(3):
        for tap_col in range(3):
            window = padded[tap_row : tap_row + row_count, tap_col : tap_col + col_count].reshape(
                row_count * col_count, -1
            )
            if input_float:
                tap_list.append(
                    jnp.einsum(
                        "pc,pd->cd",
                        window.astype(jnp.float32),
                        flat_delta,
                        precision=lax.Precision.HIGHEST,
                    )
                )
            else:
                tap_list.append(
                    jnp.einsum("pc,pd->cd", window, flat_delta, preferred_element_type=jnp.float32)
                )
    return jnp.stack(tap_list).reshape(3, 3, channels, channels)


def shards(frames, offsets, weight, bias, cotangent):
    tile_rows, tile_cols, channels = (frames.shape[2], frames.shape[3], frames.shape[4])
    border_width = MAXOFF + RAD
    row_start = lax.axis_index("row") * tile_rows
    col_start = lax.axis_index("col") * tile_cols
    inv_root = channels ** (-0.5)
    bordered = with_halo(frames, (("row", 2), ("col", 3)), 1)
    first_pad = bordered[0, 0]
    second_pad = bordered[0, 1]
    pre_one = convolve(first_pad, weight, bias, tile_rows, tile_cols)
    pre_two = convolve(second_pad, weight, bias, tile_rows, tile_cols)
    feat_two = jnp.maximum(pre_two, 0.0).astype(jnp.bfloat16)
    padded_two = with_halo(feat_two, (("row", 0), ("col", 1)), border_width)
    feat_one = jnp.maximum(pre_one, 0.0).astype(jnp.bfloat16)
    sub_rows = min(tile_rows, BLK)
    gradient_second_padded = jnp.zeros(
        (tile_rows + 2 * border_width, tile_cols + 2 * border_width, channels), jnp.float32
    )
    zero_index = jnp.zeros((), jnp.int32)
    block_row = (row_start + 0) // BLK
    block_col = (col_start + 0) // BLK
    shift_pair = offsets[0, block_row, block_col]
    start = (0 + shift_pair[0] + MAXOFF, 0 + shift_pair[1] + MAXOFF, zero_index)
    window_two = lax.dynamic_slice(padded_two, start, (sub_rows + 2 * RAD, BLK + 2 * RAD, channels))
    corr_pieces = block_scores(feat_one, window_two) * inv_root
    cot_block = cotangent[0, :, 0:sub_rows, 0:BLK]
    grad_block, grad_window = block_grads(cot_block, feat_one, window_two)
    grad_pieces = grad_block * inv_root
    gradient_second_padded = lax.dynamic_update_slice(
        gradient_second_padded, grad_window * inv_root, start
    )
    corr = corr_pieces.astype(jnp.bfloat16)[None]
    carried_state = jnp.concatenate(
        [gradient_second_padded[:border_width], gradient_second_padded[-border_width:]], axis=0
    )
    incoming_block = with_halo(
        carried_state.astype(jnp.bfloat16), (("row", 0),), border_width
    ).astype(carried_state.dtype)
    central_index = gradient_second_padded[border_width : border_width + tile_rows]
    central_index = central_index.at[:border_width].add(incoming_block[:border_width])
    central_index = central_index.at[tile_rows - border_width :].add(
        incoming_block[3 * border_width :]
    )
    carried_state = jnp.concatenate(
        [central_index[:, :border_width], central_index[:, -border_width:]], axis=1
    )
    incoming_block = with_halo(
        carried_state.astype(jnp.bfloat16), (("col", 1),), border_width
    ).astype(carried_state.dtype)
    center = central_index[:, border_width : border_width + tile_cols]
    center = center.at[:, :border_width].add(incoming_block[:, :border_width])
    center = center.at[:, tile_cols - border_width :].add(incoming_block[:, 3 * border_width :])
    delta_two = jnp.where(pre_two > 0, center, 0.0)
    delta_one = jnp.where(pre_one > 0, grad_pieces, 0.0).astype(jnp.bfloat16)
    grad_w = weight_terms(first_pad, delta_one, False) + weight_terms(second_pad, delta_two, True)
    grad_b = jnp.sum(delta_one.astype(jnp.float32), axis=(0, 1)) + jnp.sum(delta_two, axis=(0, 1))
    grad_w, grad_b = lax.psum((grad_w, grad_b), ("row", "col", "pair"))
    return (corr, grad_w, grad_b)


def solution(mesh):
    return jax.shard_map(
        shards,
        mesh=mesh,
        in_specs=(
            P("pair", None, "row", "col", None),
            P("pair", None, None, None),
            P(),
            P(),
            P("pair", None, "row", "col"),
        ),
        out_specs=(P("pair", None, "row", "col"), P(), P()),
        check_vma=False,
    )
```

profile of v0, /device:TPU:0, one launch (start us, length us, event | category | flops | bytes accessed | tf_op | source)
XLA Modules:
  0.0 254.6 jit_solution(12736524838833006585)
XLA Ops:
  7.2 0.8 fusion.142
  8.0 2.3 collective-permute-start
  10.4 1.3 collective-permute-start.1
  11.7 1.2 copy.31
  13.0 1.1 constant_dynamic-update-slice_fusion.1
  14.1 1.5 collective-permute-done.1
  15.6 3.4 %collective-permute-start.2 = (bf16[1,2,18,1,256]{4,3,2,1,0:T(2,128)(2,1)S(1)}, bf16[1,2,18,1,256]{4,3,2,1,0:T(2,128)(2,1)S(1)}, u32[]{:S(2)}, u32[]{:S(2)}) collective-permute-start(bf16[1,2,18,1,256]{4,3,2,1,0:T(2,128)(2,1)S(1)} %get-tuple-element.176), channel_id=1, source_target_pairs={{0,4},{1,5},{2,6},{3,7},{8,12},{9,13},{10,14},{11,15},{16,20},{17,... | collective-permute-start | bytes 55304 | tf_op jit(solution)/shard_map/ppermute | solution.py:19
  19.1 1.3 collective-permute-start.3
  20.4 0.6 fusion.147
  22.2 0.3 reshape.637
  23.0 0.3 reshape.639
  30.8 0.4 pad_maximum_fusion
  31.3 1.6 fusion.144
  33.0 1.1 fusion.79
  36.3 0.7 copy-done.1
  40.0 1.0 broadcast_multiply_fusion
  41.2 9.8 %dynamic_update_slice.3 = f32[40,56,256]{2,1,0:T(8,128)S(1)} dynamic-update-slice(f32[40,56,256]{2,1,0:T(8,128)S(1)} %broadcast_in_dim.4, f32[24,40,256]{2,1,0:T(8,128)} %broadcast_multiply_fusion, s32[]{:T(128)S(6)} %select_n.33, s32[]{:T(128)S(6)} %select_n.34, s32[]{:T(128)} %constant.386.clone.1) | dynamic-update-slice | bytes 1966084 | tf_op jit(solution)/shard_map/dynamic_update_slice | solution.py:154
  51.2 4.4 %collective-permute-start.8 = (bf16[12,56,256]{2,1,0:T(8,128)(2,1)S(1)}, bf16[12,56,256]{2,1,0:T(8,128)(2,1)S(1)}, u32[]{:S(2)}, u32[]{:S(2)}) collective-permute-start(bf16[12,56,256]{2,1,0:T(8,128)(2,1)S(1)} %get-tuple-element.170), channel_id=1, source_target_pairs={{0,8},{8,16},{16,24},{1,9},{9,17},{17,25},{2,10},{10,18},{18,26},{... | collective-permute-start | bytes 1032200 | tf_op jit(solution)/shard_map/ppermute | solution.py:19
  55.7 1.5 collective-permute-start.9
  58.9 0.4 copy-done.24
  59.9 4.0 %collective-permute-start.10 = (bf16[16,12,256]{2,1,0:T(8,128)(2,1)S(1)}, bf16[16,12,256]{2,1,0:T(8,128)(2,1)S(1)}, u32[]{:S(2)}, u32[]{:S(2)}) collective-permute-start(bf16[16,12,256]{2,1,0:T(8,128)(2,1)S(1)} %get-tuple-element.181), channel_id=1, source_target_pairs={{0,4},{1,5},{2,6},{3,7},{8,12},{9,13},{10,14},{11,15},{16,20},{17,... | collective-permute-start | bytes 294920 | tf_op jit(solution)/shard_map/ppermute | solution.py:19
  64.0 1.3 collective-permute-start.11
  65.6 0.9 collective-permute-done.10
  66.4 4.4 %collective-permute-done.11 = bf16[16,12,256]{2,1,0:T(8,128)(2,1)S(1)} collective-permute-done((bf16[16,12,256]{2,1,0:T(8,128)(2,1)S(1)}, bf16[16,12,256]{2,1,0:T(8,128)(2,1)S(1)}, u32[]{:S(2)}, u32[]{:S(2)}) %collective-permute-start.11) | collective-permute-done | bytes 98336 | tf_op jit(solution)/shard_map/ppermute | solution.py:21
  70.9 0.4 scatter-add.61
  71.9 5.9 %collective-permute-start.4 = (bf16[12,32,256]{2,1,0:T(8,128)(2,1)S(1)}, bf16[12,32,256]{2,1,0:T(8,128)(2,1)S(1)}, u32[]{:S(2)}, u32[]{:S(2)}) collective-permute-start(bf16[12,32,256]{2,1,0:T(8,128)(2,1)S(1)} %get-tuple-element.210), channel_id=1, source_target_pairs={{0,8},{8,16},{16,24},{1,9},{9,17},{17,25},{2,10},{10,18},{18,26},{... | collective-permute-start | bytes 589832 | tf_op jit(solution)/shard_map/ppermute | solution.py:19
  77.8 1.3 collective-permute-start.5
  79.1 0.5 fusion.19
  79.6 0.5 fusion.18
  80.1 0.5 fusion.17
  80.6 0.5 fusion.16
  81.1 0.5 fusion.15
  81.6 0.5 fusion.14
  82.1 0.5 fusion.13
  82.6 0.5 fusion.12
  83.4 1.8 collective-permute-start.6
  85.2 1.3 collective-permute-start.7
  86.5 0.5 fusion.11
  87.0 4.4 %collective-permute-done.6 = bf16[40,12,256]{2,1,0:T(8,128)(2,1)S(1)} collective-permute-done((bf16[40,12,256]{2,1,0:T(8,128)(2,1)S(1)}, bf16[40,12,256]{2,1,0:T(8,128)(2,1)S(1)}, u32[]{:S(2)}, u32[]{:S(2)}) %collective-permute-start.6) | collective-permute-done | bytes 245792 | tf_op jit(solution)/shard_map/ppermute | solution.py:19
  91.4 4.7 %collective-permute-done.7 = bf16[40,12,256]{2,1,0:T(8,128)(2,1)S(1)} collective-permute-done((bf16[40,12,256]{2,1,0:T(8,128)(2,1)S(1)}, bf16[40,12,256]{2,1,0:T(8,128)(2,1)S(1)}, u32[]{:S(2)}, u32[]{:S(2)}) %collective-permute-start.7) | collective-permute-done | bytes 245792 | tf_op jit(solution)/shard_map/ppermute | solution.py:21
  96.1 1.4 fusion.32
  97.7 0.9 fusion.39
  105.5 1.7 add.331
  107.2 0.9 copy-done.22
  114.7 1.0 copy.41
  115.7 40.9 %psum.15 = f32[256]{0:T(256)} all-reduce(f32[256]{0:T(256)S(1)} %add.333), channel_id=1, replica_groups=mesh['row'=4,'col'=2,'pair'=4] {'row','col','pair'}, use_global_device_ids=true, to_apply=%region_3.4 | all-reduce | flops 256 | bytes 2048 | tf_op jit(solution)/shard_map/psum | solution.py:182
  156.6 87.9 %all-reduce.30.cloned.1.call-done = f32[3,3,256,256]{3,2,1,0:T(8,128)} async-done(((f32[3,3,256,256]{3,2,1,0:T(8,128)}), f32[3,3,256,256]{3,2,1,0:T(8,128)}) %all-reduce.30.cloned.1.call-update) | async-done | bytes 2359312 | tf_op jit(solution)/shard_map/psum | solution.py:182
  244.5 3.2 %copy.91 = f32[3,3,256,256]{3,2,1,0:T(8,128)} copy(f32[3,3,256,256]{3,2,1,0:T(8,128)} %all-reduce.30.cloned.1.call-done) | data formatting | bytes 4718592
  (245 shorter events, 28.3 us)
Async XLA Ops:
  7.2 5.8 %copy-start = (s32[1,2,2,2]{3,2,1,0:T(2,128)S(1)}, s32[1,2,2,2]{3,2,1,0:T(2,128)}, u32[]{:S(2)}) copy-start(s32[1,2,2,2]{3,2,1,0:T(2,128)} %param.32) | copy-start | bytes 100
  7.2 237.3 %all-reduce.30.cloned.1.call-start = ((), (), s32[]{:S(2)}) async-start(), calls=%async_computation | async-start | bytes 4718592 | tf_op jit(solution)/shard_map/psum | solution.py:182
  8.0 5.0 %collective-permute-start = (bf16[1,2,1,32,256]{4,3,2,1,0:T(8,128)(2,1)S(1)}, bf16[1,2,1,32,256]{4,3,2,1,0:T(8,128)(2,1)S(1)}, u32[]{:S(2)}, u32[]{:S(2)}) collective-permute-start(bf16[1,2,1,32,256]{4,3,2,1,0:T(8,128)(2,1)S(1)} %get-tuple-element.180), channel_id=1, source_target_pairs={{0,8},{8,16},{16,24},{1,9},{9,17},{17,25},{2,10},{10,18},{18,26},{... | collective-permute-start | bytes 98312 | tf_op jit(solution)/shard_map/ppermute | solution.py:19
  10.4 5.2 %collective-permute-start.1 = (bf16[1,2,1,32,256]{4,3,2,1,0:T(8,128)(2,1)S(1)}, bf16[1,2,1,32,256]{4,3,2,1,0:T(8,128)(2,1)S(1)}, u32[]{:S(2)}, u32[]{:S(2)}) collective-permute-start(bf16[1,2,1,32,256]{4,3,2,1,0:T(8,128)(2,1)S(1)} %get-tuple-element.179), channel_id=1, source_target_pairs={{8,0},{16,8},{24,16},{9,1},{17,9},{25,17},{10,2},{18,10},{26,18},{... | collective-permute-start | bytes 98312 | tf_op jit(solution)/shard_map/ppermute | solution.py:21
  15.6 15.1 %collective-permute-start.2 = (bf16[1,2,18,1,256]{4,3,2,1,0:T(2,128)(2,1)S(1)}, bf16[1,2,18,1,256]{4,3,2,1,0:T(2,128)(2,1)S(1)}, u32[]{:S(2)}, u32[]{:S(2)}) collective-permute-start(bf16[1,2,18,1,256]{4,3,2,1,0:T(2,128)(2,1)S(1)} %get-tuple-element.176), channel_id=1, source_target_pairs={{0,4},{1,5},{2,6},{3,7},{8,12},{9,13},{10,14},{11,15},{16,20},{17,... | collective-permute-start | bytes 55304 | tf_op jit(solution)/shard_map/ppermute | solution.py:19
  19.1 11.7 %collective-permute-start.3 = (bf16[1,2,18,1,256]{4,3,2,1,0:T(2,128)(2,1)S(1)}, bf16[1,2,18,1,256]{4,3,2,1,0:T(2,128)(2,1)S(1)}, u32[]{:S(2)}, u32[]{:S(2)}) collective-permute-start(bf16[1,2,18,1,256]{4,3,2,1,0:T(2,128)(2,1)S(1)} %get-tuple-element.177), channel_id=1, source_target_pairs={{4,0},{5,1},{6,2},{7,3},{12,8},{13,9},{14,10},{15,11},{20,16},{21,... | collective-permute-start | bytes 55304 | tf_op jit(solution)/shard_map/ppermute | solution.py:21
  22.5 14.8 %copy-start.10 = (bf16[16,32,41]{2,1,0:T(8,128)(2,1)}, bf16[16,32,41]{2,1,0:T(8,128)(2,1)S(1)}, u32[]{:S(2)}) copy-start(bf16[16,32,41]{2,1,0:T(8,128)(2,1)S(1)} %reshape.637) | copy-start | bytes 125956
  23.3 14.3 %copy-start.6 = (bf16[16,32,41]{2,1,0:T(8,128)(2,1)}, bf16[16,32,41]{2,1,0:T(8,128)(2,1)S(1)}, u32[]{:S(2)}) copy-start(bf16[16,32,41]{2,1,0:T(8,128)(2,1)S(1)} %reshape.639) | copy-start | bytes 125956
  24.1 13.9 %copy-start.8 = (bf16[16,32,41]{2,1,0:T(8,128)(2,1)}, bf16[16,32,41]{2,1,0:T(8,128)(2,1)S(1)}, u32[]{:S(2)}) copy-start(bf16[16,32,41]{2,1,0:T(8,128)(2,1)S(1)} %reshape.641) | copy-start | bytes 125956
  25.0 13.4 %copy-start.12 = (bf16[16,32,41]{2,1,0:T(8,128)(2,1)}, bf16[16,32,41]{2,1,0:T(8,128)(2,1)S(1)}, u32[]{:S(2)}) copy-start(bf16[16,32,41]{2,1,0:T(8,128)(2,1)S(1)} %reshape.643) | copy-start | bytes 125956
  25.8 12.9 %copy-start.14 = (bf16[16,32,41]{2,1,0:T(8,128)(2,1)}, bf16[16,32,41]{2,1,0:T(8,128)(2,1)S(1)}, u32[]{:S(2)}) copy-start(bf16[16,32,41]{2,1,0:T(8,128)(2,1)S(1)} %reshape.645) | copy-start | bytes 125956
  26.6 12.4 %copy-start.16 = (bf16[16,32,41]{2,1,0:T(8,128)(2,1)}, bf16[16,32,41]{2,1,0:T(8,128)(2,1)S(1)}, u32[]{:S(2)}) copy-start(bf16[16,32,41]{2,1,0:T(8,128)(2,1)S(1)} %reshape.647) | copy-start | bytes 125956
  27.4 12.0 %copy-start.18 = (bf16[16,32,41]{2,1,0:T(8,128)(2,1)}, bf16[16,32,41]{2,1,0:T(8,128)(2,1)S(1)}, u32[]{:S(2)}) copy-start(bf16[16,32,41]{2,1,0:T(8,128)(2,1)S(1)} %reshape.649) | copy-start | bytes 125956
  28.2 11.5 %copy-start.20 = (bf16[16,32,41]{2,1,0:T(8,128)(2,1)}, bf16[16,32,41]{2,1,0:T(8,128)(2,1)S(1)}, u32[]{:S(2)}) copy-start(bf16[16,32,41]{2,1,0:T(8,128)(2,1)S(1)} %reshape.651) | copy-start | bytes 125956
  31.3 1.7 copy-start.3
  35.5 0.7 copy-start.31
  36.2 0.8 copy-start.1
  51.0 6.1 %copy-start.4 = (bf16[3,3,256,256]{3,2,1,0:T(8,128)(2,1)S(1)}, bf16[3,3,256,256]{3,2,1,0:T(8,128)(2,1)}, u32[]{:S(2)}) copy-start(bf16[3,3,256,256]{3,2,1,0:T(8,128)(2,1)} %param.33) | copy-start | bytes 3538948
  51.0 6.1 %copy-start.5 = (f32[512,256]{1,0:T(8,128)S(1)}, f32[512,256]{1,0:T(8,128)}, u32[]{:S(2)}) copy-start(f32[512,256]{1,0:T(8,128)} %fusion.79) | copy-start | bytes 1572868
  51.0 6.1 %copy-start.30 = (bf16[16,32,256]{2,1,0:T(8,128)(2,1)S(1)}, bf16[16,32,256]{2,1,0:T(8,128)(2,1)}, u32[]{:S(2)}) copy-start(bf16[16,32,256]{2,1,0:T(8,128)(2,1)} %get-tuple-element.190) | copy-start | bytes 786436
  51.0 6.4 %copy-start.29 = (bf16[16,32,256]{2,1,0:T(8,128)(2,1)S(1)}, bf16[16,32,256]{2,1,0:T(8,128)(2,1)}, u32[]{:S(2)}) copy-start(bf16[16,32,256]{2,1,0:T(8,128)(2,1)} %get-tuple-element.189) | copy-start | bytes 786436
  51.2 6.5 %copy-start.28 = (bf16[16,32,256]{2,1,0:T(8,128)(2,1)S(1)}, bf16[16,32,256]{2,1,0:T(8,128)(2,1)}, u32[]{:S(2)}) copy-start(bf16[16,32,256]{2,1,0:T(8,128)(2,1)} %get-tuple-element.188) | copy-start | bytes 786436
  51.2 6.7 %copy-start.27 = (bf16[16,32,256]{2,1,0:T(8,128)(2,1)S(1)}, bf16[16,32,256]{2,1,0:T(8,128)(2,1)}, u32[]{:S(2)}) copy-start(bf16[16,32,256]{2,1,0:T(8,128)(2,1)} %get-tuple-element.187) | copy-start | bytes 786436
  51.2 8.3 %collective-permute-start.8 = (bf16[12,56,256]{2,1,0:T(8,128)(2,1)S(1)}, bf16[12,56,256]{2,1,0:T(8,128)(2,1)S(1)}, u32[]{:S(2)}, u32[]{:S(2)}) collective-permute-start(bf16[12,56,256]{2,1,0:T(8,128)(2,1)S(1)} %get-tuple-element.170), channel_id=1, source_target_pairs={{0,8},{8,16},{16,24},{1,9},{9,17},{17,25},{2,10},{10,18},{18,26},{... | collective-permute-start | bytes 1032200 | tf_op jit(solution)/shard_map/ppermute | solution.py:19
  55.7 3.9 %collective-permute-start.9 = (bf16[12,56,256]{2,1,0:T(8,128)(2,1)S(1)}, bf16[12,56,256]{2,1,0:T(8,128)(2,1)S(1)}, u32[]{:S(2)}, u32[]{:S(2)}) collective-permute-start(bf16[12,56,256]{2,1,0:T(8,128)(2,1)S(1)} %get-tuple-element.171), channel_id=1, source_target_pairs={{8,0},{16,8},{24,16},{9,1},{17,9},{25,17},{10,2},{18,10},{26,18},{... | collective-permute-start | bytes 1032200 | tf_op jit(solution)/shard_map/ppermute | solution.py:21
  57.4 1.0 copy-start.26
  57.7 1.0 copy-start.25
  58.4 1.0 copy-start.24
  59.7 5.6 %copy-start.23 = (bf16[16,32,256]{2,1,0:T(8,128)(2,1)S(1)}, bf16[16,32,256]{2,1,0:T(8,128)(2,1)}, u32[]{:S(2)}) copy-start(bf16[16,32,256]{2,1,0:T(8,128)(2,1)} %get-tuple-element.183) | copy-start | bytes 786436
  59.9 6.5 %collective-permute-start.10 = (bf16[16,12,256]{2,1,0:T(8,128)(2,1)S(1)}, bf16[16,12,256]{2,1,0:T(8,128)(2,1)S(1)}, u32[]{:S(2)}, u32[]{:S(2)}) collective-permute-start(bf16[16,12,256]{2,1,0:T(8,128)(2,1)S(1)} %get-tuple-element.181), channel_id=1, source_target_pairs={{0,4},{1,5},{2,6},{3,7},{8,12},{9,13},{10,14},{11,15},{16,20},{17,... | collective-permute-start | bytes 294920 | tf_op jit(solution)/shard_map/ppermute | solution.py:19
  64.0 6.9 %collective-permute-start.11 = (bf16[16,12,256]{2,1,0:T(8,128)(2,1)S(1)}, bf16[16,12,256]{2,1,0:T(8,128)(2,1)S(1)}, u32[]{:S(2)}, u32[]{:S(2)}) collective-permute-start(bf16[16,12,256]{2,1,0:T(8,128)(2,1)S(1)} %get-tuple-element.182), channel_id=1, source_target_pairs={{4,0},{5,1},{6,2},{7,3},{12,8},{13,9},{14,10},{15,11},{20,16},{21,... | collective-permute-start | bytes 294920 | tf_op jit(solution)/shard_map/ppermute | solution.py:21
  71.9 11.2 %collective-permute-start.4 = (bf16[12,32,256]{2,1,0:T(8,128)(2,1)S(1)}, bf16[12,32,256]{2,1,0:T(8,128)(2,1)S(1)}, u32[]{:S(2)}, u32[]{:S(2)}) collective-permute-start(bf16[12,32,256]{2,1,0:T(8,128)(2,1)S(1)} %get-tuple-element.210), channel_id=1, source_target_pairs={{0,8},{8,16},{16,24},{1,9},{9,17},{17,25},{2,10},{10,18},{18,26},{... | collective-permute-start | bytes 589832 | tf_op jit(solution)/shard_map/ppermute | solution.py:19
  77.8 5.3 %collective-permute-start.5 = (bf16[12,32,256]{2,1,0:T(8,128)(2,1)S(1)}, bf16[12,32,256]{2,1,0:T(8,128)(2,1)S(1)}, u32[]{:S(2)}, u32[]{:S(2)}) collective-permute-start(bf16[12,32,256]{2,1,0:T(8,128)(2,1)S(1)} %get-tuple-element.211), channel_id=1, source_target_pairs={{8,0},{16,8},{24,16},{9,1},{17,9},{25,17},{10,2},{18,10},{26,18},{... | collective-permute-start | bytes 589832 | tf_op jit(solution)/shard_map/ppermute | solution.py:21
  83.2 14.2 %copy-start.11 = (bf16[16,32,41]{2,1,0:T(8,128)(2,1)S(1)}, bf16[16,32,41]{2,1,0:T(8,128)(2,1)}, u32[]{:S(2)}) copy-start(bf16[16,32,41]{2,1,0:T(8,128)(2,1)} %copy-done.10) | copy-start | bytes 125956
  83.4 8.1 %collective-permute-start.6 = (bf16[40,12,256]{2,1,0:T(8,128)(2,1)S(1)}, bf16[40,12,256]{2,1,0:T(8,128)(2,1)S(1)}, u32[]{:S(2)}, u32[]{:S(2)}) collective-permute-start(bf16[40,12,256]{2,1,0:T(8,128)(2,1)S(1)} %get-tuple-element.175), channel_id=1, source_target_pairs={{0,4},{1,5},{2,6},{3,7},{8,12},{9,13},{10,14},{11,15},{16,20},{17,... | collective-permute-start | bytes 737288 | tf_op jit(solution)/shard_map/ppermute | solution.py:19
  85.2 10.9 %collective-permute-start.7 = (bf16[40,12,256]{2,1,0:T(8,128)(2,1)S(1)}, bf16[40,12,256]{2,1,0:T(8,128)(2,1)S(1)}, u32[]{:S(2)}, u32[]{:S(2)}) collective-permute-start(bf16[40,12,256]{2,1,0:T(8,128)(2,1)S(1)} %get-tuple-element.174), channel_id=1, source_target_pairs={{4,0},{5,1},{6,2},{7,3},{12,8},{13,9},{14,10},{15,11},{20,16},{21,... | collective-permute-start | bytes 737288 | tf_op jit(solution)/shard_map/ppermute | solution.py:21
  99.5 1.1 copy-start.7
  100.0 0.9 copy-start.9
  100.4 0.9 copy-start.13
  100.7 0.9 copy-start.15
  100.9 0.9 copy-start.17
  101.3 0.9 copy-start.19
  101.6 1.1 copy-start.2
  101.6 1.1 copy-start.21
  107.2 0.9 copy-start.22
Sparse Core Ops, SparseCore 0:
  107.3 137.1 all-reduce.29
where the time goes:
time: 255 us
  waiting for transfers between devices  104 us (41%)
  blocking collectives  40.9 us (16%)
  local copies, waits for them, and re-layouts  37.2 us (15%)
  starting transfers between devices  29.9 us (12%)
  matrix products  19.1 us (7%)
  between operations  18.3 us (7%)
  other arithmetic  5.37 us (2%)
    psum x1, waiting for transfers between devices, shards(): grad_w, grad_b = lax.psum((grad_w, grad_b), ('row', 'col', 'pair'))  87.9 us
    psum x1, blocking collectives, shards(): grad_w, grad_b = lax.psum((grad_w, grad_b), ('row', 'col', 'pair'))  40.9 us
    ppermute x6, starting transfers between devices, with_halo(): lax.ppermute(tail, axis, [(i, (i + 1) % count) for i in range(ends)])  21.9 us
    unnamed x86, local copies, waits for them, and re-layouts  11.7 us
    ppermute x6, waiting for transfers between devices, with_halo(): lax.ppermute(head, axis, [((i + 1) % count, i) for i in range(ends)])  10.5 us
    dynamic_update_slice x1, local copies, waits for them, and re-layouts, shards(): lax.dynamic_update_slice(gradient_second_padded, grad_window * inv_root,...  9.84 us
    ppermute x6, starting transfers between devices, with_halo(): lax.ppermute(head, axis, [((i + 1) % count, i) for i in range(ends)])  7.93 us
    ppermute x6, waiting for transfers between devices, with_halo(): lax.ppermute(tail, axis, [(i, (i + 1) % count) for i in range(ends)])  5.34 us
  transfers between devices with their start and end apart: 13, of which 6 were waited for; matrix products, arithmetic and copies ran while one was open for 9% of the time, Pallas kernels for 0%

commit v1 on v0

--- a/solution.py
+++ b/solution.py
@@ -1,11 +1,16 @@
+import functools
+
 import jax
 import jax.numpy as jnp
 from jax import lax
+from jax.experimental import pallas as pl
+from jax.experimental.pallas import tpu as pltpu
 from jax.sharding import PartitionSpec as P
 
 BLK = 32
 RAD = 4
 MAXOFF = 8
+MESH = pl.DeviceIdType.MESH
 
 
 def with_halo(cells, sides, width):
@@ -121,6 +126,145 @@
                     jnp.einsum("pc,pd->cd", window, flat_delta, preferred_element_type=jnp.float32)
                 )
     return jnp.stack(tap_list).reshape(3, 3, channels, channels)
+
+
+def exchange_plan():
+    sizes = {axis: lax.axis_size(axis) for axis in ("row", "col", "pair")}
+    bits = {
+        axis: [1 << place for place in range(size.bit_length() - 1)]
+        for axis, size in sizes.items()
+    }
+    near = [("row", stride) for stride in bits["row"][:1]]
+    rest = [("row", stride) for stride in bits["row"][1:]]
+    side = [("col", stride) for stride in reversed(bits["col"])]
+    deep = [("pair", stride) for stride in reversed(bits["pair"])]
+    return [near + rest + side + deep, near + side + rest + deep]
+
+
+def sum_kernel(plans, terms, total, acc, send_half, recv_half, recv_wide, *sems):
+    rs_send, rs_recv, ag_send, ag_recv = sems
+    rows = terms.shape[1]
+    count = len(plans[0])
+    parts = range(len(plans))
+
+    def partner(step):
+        axis, stride = step
+        me = lax.axis_index(axis)
+        bit = lax.rem(me // stride, 2)
+        return bit, {axis: me + stride - 2 * stride * bit}
+
+    barrier = pltpu.get_barrier_semaphore()
+    for step in plans[0]:
+        pl.semaphore_signal(barrier, inc=1, device_id=partner(step)[1], device_id_type=MESH)
+    pl.semaphore_wait(barrier, count)
+
+    base = [0 for _ in parts]
+    trail = [[] for _ in parts]
+    waiting = [None for _ in parts]
+    sent = []
+
+    def absorb(part, place):
+        size = rows >> (place + 1)
+        copy, keep, came, wide = waiting[part]
+        copy.wait_recv()
+        source = terms if place == 0 else acc
+        add = came[...] if wide else came[...].astype(jnp.float32)
+        acc[part, pl.ds(keep, size), :] = source[part, pl.ds(keep, size), :] + add
+        base[part] = keep
+
+    for place in range(count):
+        size = rows >> (place + 1)
+        slot = rows - (rows >> place)
+        wide = place == 0 or place == count - 1
+        for part in parts:
+            if place > 0:
+                absorb(part, place - 1)
+            bit, device = partner(plans[part][place])
+            keep = pl.multiple_of(base[part] + bit * size, 16)
+            give = pl.multiple_of(base[part] + (1 - bit) * size, 16)
+            if wide:
+                source = terms if place == 0 else acc
+                first = 0 if place == 0 else rows // 2
+                src = source.at[part, pl.ds(give, size), :]
+                dst = recv_wide.at[part, pl.ds(first, size), :]
+            else:
+                send_half[part, slot : slot + size, :] = acc[part, pl.ds(give, size), :].astype(
+                    jnp.bfloat16
+                )
+                src = send_half.at[part, pl.ds(slot, size), :]
+                dst = recv_half.at[part, pl.ds(slot, size), :]
+            copy = pltpu.make_async_remote_copy(
+                src_ref=src,
+                dst_ref=dst,
+                send_sem=rs_send.at[part, place],
+                recv_sem=rs_recv.at[part, place],
+                device_id=device,
+                device_id_type=MESH,
+            )
+            copy.start()
+            sent.append(copy)
+            waiting[part] = (copy, keep, dst, wide)
+            trail[part].append(base[part])
+    for part in parts:
+        absorb(part, count - 1)
+        size = rows >> count
+        own = pl.multiple_of(base[part], 16)
+        total[part, pl.ds(own, size), :] = acc[part, pl.ds(own, size), :].astype(jnp.bfloat16)
+    for place in reversed(range(count)):
+        size = rows >> (place + 1)
+        for part in parts:
+            if place < count - 1:
+                waiting[part].wait_recv()
+            block = total.at[part, pl.ds(pl.multiple_of(base[part], 16), size), :]
+            copy = pltpu.make_async_remote_copy(
+                src_ref=block,
+                dst_ref=block,
+                send_sem=ag_send.at[part, place],
+                recv_sem=ag_recv.at[part, place],
+                device_id=partner(plans[part][place])[1],
+                device_id_type=MESH,
+            )
+            copy.start()
+            sent.append(copy)
+            waiting[part] = copy
+            base[part] = trail[part][place]
+    for part in parts:
+        waiting[part].wait_recv()
+    for copy in sent:
+        copy.wait_send()
+
+
+def padded_rows(rows):
+    devices = lax.axis_size("row") * lax.axis_size("col") * lax.axis_size("pair")
+    grain = 16 * devices
+    return (rows + grain - 1) // grain * grain
+
+
+def sum_everywhere(terms):
+    plans = exchange_plan()
+    parts, rows, lanes = terms.shape
+    count = len(plans[0])
+    semaphores = pltpu.SemaphoreType.DMA((parts, count))
+    return pl.pallas_call(
+        functools.partial(sum_kernel, plans),
+        out_shape=jax.ShapeDtypeStruct(terms.shape, jnp.bfloat16),
+        in_specs=[pl.BlockSpec(memory_space=pltpu.VMEM)],
+        out_specs=pl.BlockSpec(memory_space=pltpu.VMEM),
+        scratch_shapes=[
+            pltpu.VMEM(terms.shape, jnp.float32),
+            pltpu.VMEM(terms.shape, jnp.bfloat16),
+            pltpu.VMEM(terms.shape, jnp.bfloat16),
+            pltpu.VMEM(terms.shape, jnp.float32),
+            semaphores,
+            semaphores,
+            semaphores,
+            semaphores,
+        ],
+        compiler_params=pltpu.CompilerParams(
+            collective_id=1, has_side_effects=True, vmem_limit_bytes=32 * 2**20
+        ),
+        name="sum_everywhere",
+    )(terms)
 
 
 def shards(frames, offsets, weight, bias, cotangent):
@@ -179,8 +323,13 @@
     delta_one = jnp.where(pre_one > 0, grad_pieces, 0.0).astype(jnp.bfloat16)
     grad_w = weight_terms(first_pad, delta_one, False) + weight_terms(second_pad, delta_two, True)
     grad_b = jnp.sum(delta_one.astype(jnp.float32), axis=(0, 1)) + jnp.sum(delta_two, axis=(0, 1))
-    grad_w, grad_b = lax.psum((grad_w, grad_b), ("row", "col", "pair"))
-    return (corr, grad_w, grad_b)
+    flat = jnp.concatenate([grad_w.reshape(-1, channels), grad_b[None]], axis=0)
+    rows = flat.shape[0]
+    flat = jnp.pad(flat, ((0, padded_rows(rows) - rows), (0, 0)))
+    halves = jnp.stack([flat[:, : channels // 2], flat[:, channels // 2 :]])
+    summed = sum_everywhere(halves).astype(jnp.float32)
+    summed = jnp.concatenate([summed[0, :rows], summed[1, :rows]], axis=1)
+    return (corr, summed[: rows - 1].reshape(grad_w.shape), summed[rows - 1])
 
 
 def solution(mesh):

time: 255 us -> 150 us (0.59)
  waiting for transfers between devices: 104 us -> 16.6 us
  blocking collectives: 40.9 us -> 0 us
  Pallas kernels: 0 us -> 39.1 us
  between operations: 18.3 us -> 4.95 us
  local copies, waits for them, and re-layouts: 37.2 us -> 33.1 us
    psum x1 -> x0, waiting for transfers between devices: 87.9 us -> none  [shards(): grad_w, grad_b = lax.psum((grad_w, grad_b), ('row', 'col', 'pair'))]
    psum x1 -> x0, blocking collectives: 40.9 us -> none  [shards(): grad_w, grad_b = lax.psum((grad_w, grad_b), ('row', 'col', 'pair'))]
    pallas_call x0 -> x1, Pallas kernels: none -> 39.1 us  [sum_everywhere(): pl.pallas_call(functools.partial(sum_kernel, plans), out_shape=jax.ShapeD...]
    unnamed x86 -> x85, local copies, waits for them, and re-layouts: 11.7 us -> 7.55 us
  transfers between devices with their start and end apart: 13 -> 12, of which waited for: 6 -> 6; matrix products, arithmetic and copies ran while one was open for 9% -> 9% of each run, Pallas kernels for 0% -> 0%
where the time goes in v1:
time: 150 us; the launch traced here: 149 us
  Pallas kernels  39.1 us (26%)
  local copies, waits for them, and re-layouts  33.1 us (22%)
  starting transfers between devices  30.5 us (20%)
  matrix products  18.5 us (12%)
  waiting for transfers between devices  16.6 us (11%)
  other arithmetic  6.6 us (4%)
  between operations  4.95 us (3%)
    pallas_call x1, Pallas kernels, sum_everywhere(): pl.pallas_call(functools.partial(sum_kernel, plans), out_shape=jax.ShapeD...  39.1 us
    ppermute x6, starting transfers between devices, with_halo(): lax.ppermute(tail, axis, [(i, (i + 1) % count) for i in range(ends)])  22.5 us
    ppermute x6, waiting for transfers between devices, with_halo(): lax.ppermute(head, axis, [((i + 1) % count, i) for i in range(ends)])  12.8 us
    dynamic_update_slice x1, local copies, waits for them, and re-layouts, shards(): lax.dynamic_update_slice(gradient_second_padded, grad_window * inv_root,...  9.61 us
    ppermute x6, starting transfers between devices, with_halo(): lax.ppermute(head, axis, [((i + 1) % count, i) for i in range(ends)])  7.93 us
    unnamed x85, local copies, waits for them, and re-layouts  7.55 us
    dot_general x18, matrix products, convolve(): jnp.dot(window, weight[tap_row, tap_col], preferred_element_type=jnp.floa...  4.89 us
    dot_general x9, matrix products, weight_terms(): jnp.einsum('pc,pd->cd', window.astype(jnp.float32), flat_delta, precision...  4.44 us
  transfers between devices with their start and end apart: 12, of which 6 were waited for; matrix products, arithmetic and copies ran while one was open for 9% of the time, Pallas kernels for 0%

profile of v1, /device:TPU:0, one launch (start us, length us, event | category | flops | bytes accessed | tf_op | source)
XLA Modules:
  0.0 149.3 jit_solution(17229278114827321598)
XLA Ops:
  0.6 0.8 fusion.143
  1.4 2.3 %collective-permute-start = (bf16[1,2,1,32,256]{4,3,2,1,0:T(8,128)(2,1)S(1)}, bf16[1,2,1,32,256]{4,3,2,1,0:T(8,128)(2,1)S(1)}, u32[]{:S(2)}, u32[]{:S(2)}) collective-permute-start(bf16[1,2,1,32,256]{4,3,2,1,0:T(8,128)(2,1)S(1)} %get-tuple-element.184), channel_id=1, source_target_pairs={{0,8},{8,16},{16,24},{1,9},{9,17},{17,25},{2,10},{10,18},{18,26},{... | collective-permute-start | bytes 98312 | tf_op jit(solution)/shard_map/ppermute | solution.py:24
  3.8 1.3 collective-permute-start.1
  5.1 1.2 copy.31
  6.4 1.1 constant_dynamic-update-slice_fusion.1
  7.5 1.5 collective-permute-done.1
  9.1 3.4 %collective-permute-start.2 = (bf16[1,2,18,1,256]{4,3,2,1,0:T(2,128)(2,1)S(1)}, bf16[1,2,18,1,256]{4,3,2,1,0:T(2,128)(2,1)S(1)}, u32[]{:S(2)}, u32[]{:S(2)}) collective-permute-start(bf16[1,2,18,1,256]{4,3,2,1,0:T(2,128)(2,1)S(1)} %get-tuple-element.180), channel_id=1, source_target_pairs={{0,4},{1,5},{2,6},{3,7},{8,12},{9,13},{10,14},{11,15},{16,20},{17,... | collective-permute-start | bytes 55304 | tf_op jit(solution)/shard_map/ppermute | solution.py:24
  12.5 1.3 collective-permute-start.3
  13.8 0.6 fusion.148
  14.8 0.3 reshape.653
  15.6 0.3 reshape.655
  16.4 0.3 reshape.657
  17.2 0.3 reshape.659
  24.2 0.4 pad_maximum_fusion.1
  24.7 1.6 %fusion.145 = (bf16[16,32,256]{2,1,0:T(8,128)(2,1)}, bf16[16,32,256]{2,1,0:T(8,128)(2,1)}, bf16[16,32,256]{2,1,0:T(8,128)(2,1)}, bf16[16,32,256]{2,1,0:T(8,128)(...) fusion(bf16[18,34,256]{2,1,0:T(8,128)(2,1)S(1)} %get-tuple-elem, ...), kind=kLoop, calls=%fused_computation.261 | loop fusion | bytes 9437184 | tf_op jit(solution)/shard_map/slice | solution.py:97
  26.4 1.0 fusion.80
  29.7 0.7 copy-done.2
  33.4 1.0 broadcast_multiply_fusion
  34.6 9.6 %dynamic_update_slice.3 = f32[40,56,256]{2,1,0:T(8,128)S(1)} dynamic-update-slice(f32[40,56,256]{2,1,0:T(8,128)S(1)} %broadcast_in_dim.4, f32[24,40,256]{2,1,0:T(8,128)} %broadcast_multiply_fusion, s32[]{:T(128)S(6)} %select_n.33, s32[]{:T(128)S(6)} %select_n.34, s32[]{:T(128)} %constant.386.clone.1) | dynamic-update-slice | bytes 1966084 | tf_op jit(solution)/shard_map/dynamic_update_slice | solution.py:298
  44.4 4.4 %collective-permute-start.8 = (bf16[12,56,256]{2,1,0:T(8,128)(2,1)S(1)}, bf16[12,56,256]{2,1,0:T(8,128)(2,1)S(1)}, u32[]{:S(2)}, u32[]{:S(2)}) collective-permute-start(bf16[12,56,256]{2,1,0:T(8,128)(2,1)S(1)} %get-tuple-element.174), channel_id=1, source_target_pairs={{0,8},{8,16},{16,24},{1,9},{9,17},{17,25},{2,10},{10,18},{18,26},{... | collective-permute-start | bytes 1032200 | tf_op jit(solution)/shard_map/ppermute | solution.py:24
  48.9 1.5 collective-permute-start.9
  52.1 0.4 copy-done.24
  53.1 4.8 %collective-permute-start.10 = (bf16[16,12,256]{2,1,0:T(8,128)(2,1)S(1)}, bf16[16,12,256]{2,1,0:T(8,128)(2,1)S(1)}, u32[]{:S(2)}, u32[]{:S(2)}) collective-permute-start(bf16[16,12,256]{2,1,0:T(8,128)(2,1)S(1)} %get-tuple-element.185), channel_id=1, source_target_pairs={{0,4},{1,5},{2,6},{3,7},{8,12},{9,13},{10,14},{11,15},{16,20},{17,... | collective-permute-start | bytes 294920 | tf_op jit(solution)/shard_map/ppermute | solution.py:24
  57.9 1.3 collective-permute-start.11
  59.6 0.9 collective-permute-done.10
  60.4 4.4 %collective-permute-done.11 = bf16[16,12,256]{2,1,0:T(8,128)(2,1)S(1)} collective-permute-done((bf16[16,12,256]{2,1,0:T(8,128)(2,1)S(1)}, bf16[16,12,256]{2,1,0:T(8,128)(2,1)S(1)}, u32[]{:S(2)}, u32[]{:S(2)}) %collective-permute-start.11) | collective-permute-done | bytes 98336 | tf_op jit(solution)/shard_map/ppermute | solution.py:26
  64.9 0.4 scatter-add.61
  65.8 0.5 fusion.20
  66.3 0.5 fusion.19
  66.8 0.5 fusion.18
  67.4 0.5 fusion.17
  67.8 0.5 fusion.16
  68.3 0.5 fusion.15
  68.9 0.5 fusion.14
  69.4 6.0 %collective-permute-start.4 = (bf16[12,32,256]{2,1,0:T(8,128)(2,1)S(1)}, bf16[12,32,256]{2,1,0:T(8,128)(2,1)S(1)}, u32[]{:S(2)}, u32[]{:S(2)}) collective-permute-start(bf16[12,32,256]{2,1,0:T(8,128)(2,1)S(1)} %get-tuple-element.214), channel_id=1, source_target_pairs={{0,8},{8,16},{16,24},{1,9},{9,17},{17,25},{2,10},{10,18},{18,26},{... | collective-permute-start | bytes 589832 | tf_op jit(solution)/shard_map/ppermute | solution.py:24
  75.4 1.3 collective-permute-start.5
  76.7 0.5 fusion.13
  77.2 2.3 %collective-permute-done.5 = bf16[12,32,256]{2,1,0:T(8,128)(2,1)S(1)} collective-permute-done((bf16[12,32,256]{2,1,0:T(8,128)(2,1)S(1)}, bf16[12,32,256]{2,1,0:T(8,128)(2,1)S(1)}, u32[]{:S(2)}, u32[]{:S(2)}) %collective-permute-start.5) | collective-permute-done | bytes 196640 | tf_op jit(solution)/shard_map/ppermute | solution.py:26
  79.7 1.5 %collective-permute-start.6 = (bf16[40,12,256]{2,1,0:T(8,128)(2,1)S(1)}, bf16[40,12,256]{2,1,0:T(8,128)(2,1)S(1)}, u32[]{:S(2)}, u32[]{:S(2)}) collective-permute-start(bf16[40,12,256]{2,1,0:T(8,128)(2,1)S(1)} %get-tuple-element.179), channel_id=1, source_target_pairs={{0,4},{1,5},{2,6},{3,7},{8,12},{9,13},{10,14},{11,15},{16,20},{17,... | collective-permute-start | bytes 737288 | tf_op jit(solution)/shard_map/ppermute | solution.py:24
  81.2 1.3 collective-permute-start.7
  82.5 0.5 fusion.12
  83.0 2.9 %collective-permute-done.6 = bf16[40,12,256]{2,1,0:T(8,128)(2,1)S(1)} collective-permute-done((bf16[40,12,256]{2,1,0:T(8,128)(2,1)S(1)}, bf16[40,12,256]{2,1,0:T(8,128)(2,1)S(1)}, u32[]{:S(2)}, u32[]{:S(2)}) %collective-permute-start.6) | collective-permute-done | bytes 245792 | tf_op jit(solution)/shard_map/ppermute | solution.py:24
  85.9 4.7 %collective-permute-done.7 = bf16[40,12,256]{2,1,0:T(8,128)(2,1)S(1)} collective-permute-done((bf16[40,12,256]{2,1,0:T(8,128)(2,1)S(1)}, bf16[40,12,256]{2,1,0:T(8,128)(2,1)S(1)}, u32[]{:S(2)}, u32[]{:S(2)}) %collective-permute-start.7) | collective-permute-done | bytes 245792 | tf_op jit(solution)/shard_map/ppermute | solution.py:26
  90.6 1.4 fusion.33
  98.2 39.1 %sum_everywhere.1 = bf16[2,2560,128]{2,1,0:T(8,128)(2,1)S(1)} custom-call(f32[2,2560,128]{2,1,0:T(8,128)S(1)} %pad_maximum_fusion.terms), custom_call_target="tpu_custom_call" | custom-call | tf_op jit(solution)/shard_map/sum_everywhere/pallas_call | solution.py:248
  137.6 0.6 pad_maximum_fusion.9
  138.1 1.6 %fusion = f32[2304,256]{1,0:T(8,128)} fusion(f32[2305,128]{1,0:T(8,128)S(1)} %get-tuple-element.171, f32[2305,128]{1,0:T(8,128)S(1)} %get-tuple-element.170), kind=kLoop, calls=%fused_computation.5 | loop fusion | flops 589824 | bytes 4719616 | tf_op jit(solution)/shard_map/concatenate | solution.py:331
  148.3 1.0 copy.41
  (248 shorter events, 29.0 us)
Async XLA Ops:
  0.6 5.8 %copy-start = (s32[1,2,2,2]{3,2,1,0:T(2,128)S(1)}, s32[1,2,2,2]{3,2,1,0:T(2,128)}, u32[]{:S(2)}) copy-start(s32[1,2,2,2]{3,2,1,0:T(2,128)} %param.32) | copy-start | bytes 100
  1.4 5.0 %collective-permute-start = (bf16[1,2,1,32,256]{4,3,2,1,0:T(8,128)(2,1)S(1)}, bf16[1,2,1,32,256]{4,3,2,1,0:T(8,128)(2,1)S(1)}, u32[]{:S(2)}, u32[]{:S(2)}) collective-permute-start(bf16[1,2,1,32,256]{4,3,2,1,0:T(8,128)(2,1)S(1)} %get-tuple-element.184), channel_id=1, source_target_pairs={{0,8},{8,16},{16,24},{1,9},{9,17},{17,25},{2,10},{10,18},{18,26},{... | collective-permute-start | bytes 98312 | tf_op jit(solution)/shard_map/ppermute | solution.py:24
  3.8 5.2 %collective-permute-start.1 = (bf16[1,2,1,32,256]{4,3,2,1,0:T(8,128)(2,1)S(1)}, bf16[1,2,1,32,256]{4,3,2,1,0:T(8,128)(2,1)S(1)}, u32[]{:S(2)}, u32[]{:S(2)}) collective-permute-start(bf16[1,2,1,32,256]{4,3,2,1,0:T(8,128)(2,1)S(1)} %get-tuple-element.183), channel_id=1, source_target_pairs={{8,0},{16,8},{24,16},{9,1},{17,9},{25,17},{10,2},{18,10},{26,18},{... | collective-permute-start | bytes 98312 | tf_op jit(solution)/shard_map/ppermute | solution.py:26
  9.1 15.1 %collective-permute-start.2 = (bf16[1,2,18,1,256]{4,3,2,1,0:T(2,128)(2,1)S(1)}, bf16[1,2,18,1,256]{4,3,2,1,0:T(2,128)(2,1)S(1)}, u32[]{:S(2)}, u32[]{:S(2)}) collective-permute-start(bf16[1,2,18,1,256]{4,3,2,1,0:T(2,128)(2,1)S(1)} %get-tuple-element.180), channel_id=1, source_target_pairs={{0,4},{1,5},{2,6},{3,7},{8,12},{9,13},{10,14},{11,15},{16,20},{17,... | collective-permute-start | bytes 55304 | tf_op jit(solution)/shard_map/ppermute | solution.py:24
  12.5 11.7 %collective-permute-start.3 = (bf16[1,2,18,1,256]{4,3,2,1,0:T(2,128)(2,1)S(1)}, bf16[1,2,18,1,256]{4,3,2,1,0:T(2,128)(2,1)S(1)}, u32[]{:S(2)}, u32[]{:S(2)}) collective-permute-start(bf16[1,2,18,1,256]{4,3,2,1,0:T(2,128)(2,1)S(1)} %get-tuple-element.181), channel_id=1, source_target_pairs={{4,0},{5,1},{6,2},{7,3},{12,8},{13,9},{14,10},{15,11},{20,16},{21,... | collective-permute-start | bytes 55304 | tf_op jit(solution)/shard_map/ppermute | solution.py:26
  16.0 14.8 %copy-start.7 = (bf16[16,32,41]{2,1,0:T(8,128)(2,1)}, bf16[16,32,41]{2,1,0:T(8,128)(2,1)S(1)}, u32[]{:S(2)}) copy-start(bf16[16,32,41]{2,1,0:T(8,128)(2,1)S(1)} %reshape.655) | copy-start | bytes 125956
  16.8 14.3 %copy-start.9 = (bf16[16,32,41]{2,1,0:T(8,128)(2,1)}, bf16[16,32,41]{2,1,0:T(8,128)(2,1)S(1)}, u32[]{:S(2)}) copy-start(bf16[16,32,41]{2,1,0:T(8,128)(2,1)S(1)} %reshape.657) | copy-start | bytes 125956
  17.6 13.9 %copy-start.11 = (bf16[16,32,41]{2,1,0:T(8,128)(2,1)}, bf16[16,32,41]{2,1,0:T(8,128)(2,1)S(1)}, u32[]{:S(2)}) copy-start(bf16[16,32,41]{2,1,0:T(8,128)(2,1)S(1)} %reshape.659) | copy-start | bytes 125956
  18.4 13.4 %copy-start.13 = (bf16[16,32,41]{2,1,0:T(8,128)(2,1)}, bf16[16,32,41]{2,1,0:T(8,128)(2,1)S(1)}, u32[]{:S(2)}) copy-start(bf16[16,32,41]{2,1,0:T(8,128)(2,1)S(1)} %reshape.661) | copy-start | bytes 125956
  19.2 12.9 %copy-start.15 = (bf16[16,32,41]{2,1,0:T(8,128)(2,1)}, bf16[16,32,41]{2,1,0:T(8,128)(2,1)S(1)}, u32[]{:S(2)}) copy-start(bf16[16,32,41]{2,1,0:T(8,128)(2,1)S(1)} %reshape.663) | copy-start | bytes 125956
  20.0 12.4 %copy-start.17 = (bf16[16,32,41]{2,1,0:T(8,128)(2,1)}, bf16[16,32,41]{2,1,0:T(8,128)(2,1)S(1)}, u32[]{:S(2)}) copy-start(bf16[16,32,41]{2,1,0:T(8,128)(2,1)S(1)} %reshape.665) | copy-start | bytes 125956
  20.8 12.0 %copy-start.19 = (bf16[16,32,41]{2,1,0:T(8,128)(2,1)}, bf16[16,32,41]{2,1,0:T(8,128)(2,1)S(1)}, u32[]{:S(2)}) copy-start(bf16[16,32,41]{2,1,0:T(8,128)(2,1)S(1)} %reshape.667) | copy-start | bytes 125956
  21.6 11.5 %copy-start.21 = (bf16[16,32,41]{2,1,0:T(8,128)(2,1)}, bf16[16,32,41]{2,1,0:T(8,128)(2,1)S(1)}, u32[]{:S(2)}) copy-start(bf16[16,32,41]{2,1,0:T(8,128)(2,1)S(1)} %reshape.669) | copy-start | bytes 125956
  24.7 1.7 %copy-start.4 = (bf16[3,3,256,256]{3,2,1,0:T(8,128)(2,1)S(1)}, bf16[3,3,256,256]{3,2,1,0:T(8,128)(2,1)}, u32[]{:S(2)}) copy-start(bf16[3,3,256,256]{3,2,1,0:T(8,128)(2,1)} %param.33) | copy-start | bytes 3538948
  28.9 0.7 copy-start.31
  29.6 0.8 copy-start.2
  44.2 6.1 %copy-start.5 = (bf16[3,3,256,256]{3,2,1,0:T(8,128)(2,1)S(1)}, bf16[3,3,256,256]{3,2,1,0:T(8,128)(2,1)}, u32[]{:S(2)}) copy-start(bf16[3,3,256,256]{3,2,1,0:T(8,128)(2,1)} %param.33) | copy-start | bytes 3538948
  44.2 6.1 %copy-start.6 = (f32[512,256]{1,0:T(8,128)S(1)}, f32[512,256]{1,0:T(8,128)}, u32[]{:S(2)}) copy-start(f32[512,256]{1,0:T(8,128)} %fusion.80) | copy-start | bytes 1572868
  44.2 6.1 %copy-start.30 = (bf16[16,32,256]{2,1,0:T(8,128)(2,1)S(1)}, bf16[16,32,256]{2,1,0:T(8,128)(2,1)}, u32[]{:S(2)}) copy-start(bf16[16,32,256]{2,1,0:T(8,128)(2,1)} %get-tuple-element.194) | copy-start | bytes 786436
  44.2 6.4 %copy-start.29 = (bf16[16,32,256]{2,1,0:T(8,128)(2,1)S(1)}, bf16[16,32,256]{2,1,0:T(8,128)(2,1)}, u32[]{:S(2)}) copy-start(bf16[16,32,256]{2,1,0:T(8,128)(2,1)} %get-tuple-element.193) | copy-start | bytes 786436
  44.4 6.5 %copy-start.28 = (bf16[16,32,256]{2,1,0:T(8,128)(2,1)S(1)}, bf16[16,32,256]{2,1,0:T(8,128)(2,1)}, u32[]{:S(2)}) copy-start(bf16[16,32,256]{2,1,0:T(8,128)(2,1)} %get-tuple-element.192) | copy-start | bytes 786436
  44.4 6.7 %copy-start.27 = (bf16[16,32,256]{2,1,0:T(8,128)(2,1)S(1)}, bf16[16,32,256]{2,1,0:T(8,128)(2,1)}, u32[]{:S(2)}) copy-start(bf16[16,32,256]{2,1,0:T(8,128)(2,1)} %get-tuple-element.191) | copy-start | bytes 786436
  44.4 8.3 %collective-permute-start.8 = (bf16[12,56,256]{2,1,0:T(8,128)(2,1)S(1)}, bf16[12,56,256]{2,1,0:T(8,128)(2,1)S(1)}, u32[]{:S(2)}, u32[]{:S(2)}) collective-permute-start(bf16[12,56,256]{2,1,0:T(8,128)(2,1)S(1)} %get-tuple-element.174), channel_id=1, source_target_pairs={{0,8},{8,16},{16,24},{1,9},{9,17},{17,25},{2,10},{10,18},{18,26},{... | collective-permute-start | bytes 1032200 | tf_op jit(solution)/shard_map/ppermute | solution.py:24
  48.9 3.9 %collective-permute-start.9 = (bf16[12,56,256]{2,1,0:T(8,128)(2,1)S(1)}, bf16[12,56,256]{2,1,0:T(8,128)(2,1)S(1)}, u32[]{:S(2)}, u32[]{:S(2)}) collective-permute-start(bf16[12,56,256]{2,1,0:T(8,128)(2,1)S(1)} %get-tuple-element.175), channel_id=1, source_target_pairs={{8,0},{16,8},{24,16},{9,1},{17,9},{25,17},{10,2},{18,10},{26,18},{... | collective-permute-start | bytes 1032200 | tf_op jit(solution)/shard_map/ppermute | solution.py:26
  50.6 1.0 copy-start.26
  50.9 1.0 copy-start.25
  51.6 1.0 copy-start.24
  52.9 6.4 %copy-start.23 = (bf16[16,32,256]{2,1,0:T(8,128)(2,1)S(1)}, bf16[16,32,256]{2,1,0:T(8,128)(2,1)}, u32[]{:S(2)}) copy-start(bf16[16,32,256]{2,1,0:T(8,128)(2,1)} %get-tuple-element.187) | copy-start | bytes 786436
  53.1 7.3 %collective-permute-start.10 = (bf16[16,12,256]{2,1,0:T(8,128)(2,1)S(1)}, bf16[16,12,256]{2,1,0:T(8,128)(2,1)S(1)}, u32[]{:S(2)}, u32[]{:S(2)}) collective-permute-start(bf16[16,12,256]{2,1,0:T(8,128)(2,1)S(1)} %get-tuple-element.185), channel_id=1, source_target_pairs={{0,4},{1,5},{2,6},{3,7},{8,12},{9,13},{10,14},{11,15},{16,20},{17,... | collective-permute-start | bytes 294920 | tf_op jit(solution)/shard_map/ppermute | solution.py:24
  57.9 6.9 %collective-permute-start.11 = (bf16[16,12,256]{2,1,0:T(8,128)(2,1)S(1)}, bf16[16,12,256]{2,1,0:T(8,128)(2,1)S(1)}, u32[]{:S(2)}, u32[]{:S(2)}) collective-permute-start(bf16[16,12,256]{2,1,0:T(8,128)(2,1)S(1)} %get-tuple-element.186), channel_id=1, source_target_pairs={{4,0},{5,1},{6,2},{7,3},{12,8},{13,9},{14,10},{15,11},{20,16},{21,... | collective-permute-start | bytes 294920 | tf_op jit(solution)/shard_map/ppermute | solution.py:26
  69.4 7.8 %collective-permute-start.4 = (bf16[12,32,256]{2,1,0:T(8,128)(2,1)S(1)}, bf16[12,32,256]{2,1,0:T(8,128)(2,1)S(1)}, u32[]{:S(2)}, u32[]{:S(2)}) collective-permute-start(bf16[12,32,256]{2,1,0:T(8,128)(2,1)S(1)} %get-tuple-element.214), channel_id=1, source_target_pairs={{0,8},{8,16},{16,24},{1,9},{9,17},{17,25},{2,10},{10,18},{18,26},{... | collective-permute-start | bytes 589832 | tf_op jit(solution)/shard_map/ppermute | solution.py:24
  75.4 4.1 %collective-permute-start.5 = (bf16[12,32,256]{2,1,0:T(8,128)(2,1)S(1)}, bf16[12,32,256]{2,1,0:T(8,128)(2,1)S(1)}, u32[]{:S(2)}, u32[]{:S(2)}) collective-permute-start(bf16[12,32,256]{2,1,0:T(8,128)(2,1)S(1)} %get-tuple-element.215), channel_id=1, source_target_pairs={{8,0},{16,8},{24,16},{9,1},{17,9},{25,17},{10,2},{18,10},{26,18},{... | collective-permute-start | bytes 589832 | tf_op jit(solution)/shard_map/ppermute | solution.py:26
  79.6 12.4 %copy-start.8 = (bf16[16,32,41]{2,1,0:T(8,128)(2,1)S(1)}, bf16[16,32,41]{2,1,0:T(8,128)(2,1)}, u32[]{:S(2)}) copy-start(bf16[16,32,41]{2,1,0:T(8,128)(2,1)} %copy-done.7) | copy-start | bytes 125956
  79.7 6.2 %collective-permute-start.6 = (bf16[40,12,256]{2,1,0:T(8,128)(2,1)S(1)}, bf16[40,12,256]{2,1,0:T(8,128)(2,1)S(1)}, u32[]{:S(2)}, u32[]{:S(2)}) collective-permute-start(bf16[40,12,256]{2,1,0:T(8,128)(2,1)S(1)} %get-tuple-element.179), channel_id=1, source_target_pairs={{0,4},{1,5},{2,6},{3,7},{8,12},{9,13},{10,14},{11,15},{16,20},{17,... | collective-permute-start | bytes 737288 | tf_op jit(solution)/shard_map/ppermute | solution.py:24
  81.2 9.4 %collective-permute-start.7 = (bf16[40,12,256]{2,1,0:T(8,128)(2,1)S(1)}, bf16[40,12,256]{2,1,0:T(8,128)(2,1)S(1)}, u32[]{:S(2)}, u32[]{:S(2)}) collective-permute-start(bf16[40,12,256]{2,1,0:T(8,128)(2,1)S(1)} %get-tuple-element.178), channel_id=1, source_target_pairs={{4,0},{5,1},{6,2},{7,3},{12,8},{13,9},{14,10},{15,11},{20,16},{21,... | collective-permute-start | bytes 737288 | tf_op jit(solution)/shard_map/ppermute | solution.py:26
  83.0 9.4 %copy-start.10 = (bf16[16,32,41]{2,1,0:T(8,128)(2,1)S(1)}, bf16[16,32,41]{2,1,0:T(8,128)(2,1)}, u32[]{:S(2)}) copy-start(bf16[16,32,41]{2,1,0:T(8,128)(2,1)} %copy-done.9) | copy-start | bytes 125956
  92.0 0.9 copy-start.12
  92.2 0.9 copy-start.14
  92.5 0.9 copy-start.16
  92.9 0.9 copy-start.18
  93.1 0.9 copy-start.20
  93.4 1.1 copy-start.3
  93.4 1.1 copy-start.22
  147.4 1.9 %copy-start.1 = (s32[1,2,2,2]{3,2,1,0:T(2,128)S(1)}, s32[1,2,2,2]{3,2,1,0:T(2,128)}, u32[]{:S(2)}) copy-start(s32[1,2,2,2]{3,2,1,0:T(2,128)} %param.32) | copy-start | bytes 100

commit v2 on v1

v2 whole, which is shorter than its diff:
```python
import functools

import jax
import jax.numpy as jnp
from jax import lax
from jax.experimental import pallas as pl
from jax.experimental.pallas import tpu as pltpu
from jax.sharding import PartitionSpec as P

BLK = 32
RAD = 4
MAXOFF = 8
MESH = pl.DeviceIdType.MESH


def exchange_plan():
    sizes = {axis: lax.axis_size(axis) for axis in ("row", "col", "pair")}
    bits = {
        axis: [1 << place for place in range(size.bit_length() - 1)]
        for axis, size in sizes.items()
    }
    near = [("row", stride) for stride in bits["row"][:1]]
    rest = [("row", stride) for stride in bits["row"][1:]]
    side = [("col", stride) for stride in reversed(bits["col"])]
    deep = [("pair", stride) for stride in reversed(bits["pair"])]
    return [near + rest + side + deep, near + side + rest + deep]


def sum_kernel(plans, terms, total, acc, send_half, recv_half, recv_wide, *sems):
    rs_send, rs_recv, ag_send, ag_recv = sems
    rows = terms.shape[1]
    count = len(plans[0])
    parts = range(len(plans))

    def partner(step):
        axis, stride = step
        me = lax.axis_index(axis)
        bit = lax.rem(me // stride, 2)
        return bit, {axis: me + stride - 2 * stride * bit}

    barrier = pltpu.get_barrier_semaphore()
    for step in plans[0]:
        pl.semaphore_signal(barrier, inc=1, device_id=partner(step)[1], device_id_type=MESH)
    pl.semaphore_wait(barrier, count)

    base = [0 for _ in parts]
    trail = [[] for _ in parts]
    waiting = [None for _ in parts]
    sent = []

    def absorb(part, place):
        size = rows >> (place + 1)
        copy, keep, came, wide = waiting[part]
        copy.wait_recv()
        source = terms if place == 0 else acc
        add = came[...] if wide else came[...].astype(jnp.float32)
        acc[part, pl.ds(keep, size), :] = source[part, pl.ds(keep, size), :] + add
        base[part] = keep

    for place in range(count):
        size = rows >> (place + 1)
        slot = rows - (rows >> place)
        wide = place == 0 or place == count - 1
        for part in parts:
            if place > 0:
                absorb(part, place - 1)
            bit, device = partner(plans[part][place])
            keep = pl.multiple_of(base[part] + bit * size, 16)
            give = pl.multiple_of(base[part] + (1 - bit) * size, 16)
            if wide:
                source = terms if place == 0 else acc
                first = 0 if place == 0 else rows // 2
                src = source.at[part, pl.ds(give, size), :]
                dst = recv_wide.at[part, pl.ds(first, size), :]
            else:
                send_half[part, slot : slot + size, :] = acc[part, pl.ds(give, size), :].astype(
                    jnp.bfloat16
                )
                src = send_half.at[part, pl.ds(slot, size), :]
                dst = recv_half.at[part, pl.ds(slot, size), :]
            copy = pltpu.make_async_remote_copy(
                src_ref=src,
                dst_ref=dst,
                send_sem=rs_send.at[part, place],
                recv_sem=rs_recv.at[part, place],
                device_id=device,
                device_id_type=MESH,
            )
            copy.start()
            sent.append(copy)
            waiting[part] = (copy, keep, dst, wide)
            trail[part].append(base[part])
    for part in parts:
        absorb(part, count - 1)
        size = rows >> count
        own = pl.multiple_of(base[part], 16)
        total[part, pl.ds(own, size), :] = acc[part, pl.ds(own, size), :].astype(jnp.bfloat16)
    for place in reversed(range(count)):
        size = rows >> (place + 1)
        for part in parts:
            if place < count - 1:
                waiting[part].wait_recv()
            block = total.at[part, pl.ds(pl.multiple_of(base[part], 16), size), :]
            copy = pltpu.make_async_remote_copy(
                src_ref=block,
                dst_ref=block,
                send_sem=ag_send.at[part, place],
                recv_sem=ag_recv.at[part, place],
                device_id=partner(plans[part][place])[1],
                device_id_type=MESH,
            )
            copy.start()
            sent.append(copy)
            waiting[part] = copy
            base[part] = trail[part][place]
    for part in parts:
        waiting[part].wait_recv()
    for copy in sent:
        copy.wait_send()


def padded_rows(rows):
    devices = lax.axis_size("row") * lax.axis_size("col") * lax.axis_size("pair")
    grain = 16 * devices
    return (rows + grain - 1) // grain * grain


def sum_everywhere(terms):
    plans = exchange_plan()
    parts, rows, lanes = terms.shape
    count = len(plans[0])
    semaphores = pltpu.SemaphoreType.DMA((parts, count))
    return pl.pallas_call(
        functools.partial(sum_kernel, plans),
        out_shape=jax.ShapeDtypeStruct(terms.shape, jnp.bfloat16),
        in_specs=[pl.BlockSpec(memory_space=pltpu.VMEM)],
        out_specs=pl.BlockSpec(memory_space=pltpu.VMEM),
        scratch_shapes=[
            pltpu.VMEM(terms.shape, jnp.float32),
            pltpu.VMEM(terms.shape, jnp.bfloat16),
            pltpu.VMEM(terms.shape, jnp.bfloat16),
            pltpu.VMEM(terms.shape, jnp.float32),
            semaphores,
            semaphores,
            semaphores,
            semaphores,
        ],
        compiler_params=pltpu.CompilerParams(
            collective_id=1, has_side_effects=True, vmem_limit_bytes=32 * 2**20
        ),
        name="sum_everywhere",
    )(terms)


def halo_kernel(wide, edge, frames, pad_one, pad_two, send_sem, recv_sem, own_sem):
    row, col = lax.axis_index("row"), lax.axis_index("col")
    row_count, col_count = lax.axis_size("row"), lax.axis_size("col")
    tile_rows, tile_cols = frames.shape[1], frames.shape[2]
    ways = [(down, right) for down in (0, -1, 1) for right in (0, -1, 1) if (down, right) != (0, 0)]

    def lies(down, right):
        inside_rows = (row + down >= 0) & (row + down < row_count)
        inside_cols = (col + right >= 0) & (col + right < col_count)
        return inside_rows & inside_cols

    def device(down, right):
        return {"row": row + down, "col": col + right}

    def span(step, size, halo):
        if step == 0:
            return pl.ds(0, size), pl.ds(halo, size)
        if step > 0:
            return pl.ds(size - halo, halo), pl.ds(0, halo)
        return pl.ds(0, halo), pl.ds(halo + size, halo)

    barrier = pltpu.get_barrier_semaphore()
    for way in ways:
        @pl.when(lies(*way))
        def _():
            pl.semaphore_signal(barrier, inc=1, device_id=device(*way), device_id_type=MESH)
    own = []
    for frame, (pad, halo) in enumerate(((pad_one, 1), (pad_two, wide))):
        middle = pad.at[pl.ds(halo, tile_rows), pl.ds(edge, tile_cols), :]
        own.append(pltpu.make_async_copy(frames.at[frame], middle, own_sem.at[frame]))
        own[-1].start()
    near_rows = 1 + (row > 0).astype(jnp.int32) + (row < row_count - 1).astype(jnp.int32)
    near_cols = 1 + (col > 0).astype(jnp.int32) + (col < col_count - 1).astype(jnp.int32)
    pl.semaphore_wait(barrier, near_rows * near_cols - 1)
    copies = []
    for place, way in enumerate(ways):
        for frame, (pad, halo) in enumerate(((pad_one, 1), (pad_two, wide))):
            take_rows, put_rows = span(way[0], tile_rows, halo)
            take_cols, put_cols = span(way[1], tile_cols, edge)
            copy = pltpu.make_async_remote_copy(
                src_ref=frames.at[frame, take_rows, take_cols, :],
                dst_ref=pad.at[put_rows, put_cols, :],
                send_sem=send_sem.at[place, frame],
                recv_sem=recv_sem.at[place, frame],
                device_id=device(*way),
                device_id_type=MESH,
            )
            copies.append((way, copy))
            pl.when(lies(*way))(copy.start)
    for copy in own:
        copy.wait()
    for way, copy in copies:
        pl.when(lies(-way[0], -way[1]))(copy.wait_recv)
    for way, copy in copies:
        pl.when(lies(*way))(copy.wait_send)


def gather_halos(frames, wide, edge):
    tile_rows, tile_cols, channels = frames.shape[1:]
    pads = [
        jax.ShapeDtypeStruct((tile_rows + 2 * halo, tile_cols + 2 * edge, channels), frames.dtype)
        for halo in (1, wide)
    ]
    return pl.pallas_call(
        functools.partial(halo_kernel, wide, edge),
        out_shape=pads,
        in_specs=[pl.BlockSpec(memory_space=pl.ANY)],
        out_specs=[pl.BlockSpec(memory_space=pl.ANY)] * 2,
        scratch_shapes=[
            pltpu.SemaphoreType.DMA((8, 2)),
            pltpu.SemaphoreType.DMA((8, 2)),
            pltpu.SemaphoreType.DMA((2,)),
        ],
        compiler_params=pltpu.CompilerParams(collective_id=0, has_side_effects=True),
        name="gather_halos",
    )(frames)


def tile_kernel(
    geometry, place, pad_one, pad_two, weight, bias, cot, corr, terms,
    taps_one, taps_two, pre_one, pre_two, feat_one, feat_two, delta_one, flip_one, flip_two,
    grad_two, cot_wide, corr_wide, lanes_wide,
):
    tile_rows, tile_cols, image_rows, image_cols, edge, width = geometry
    channels = bias.shape[1]
    side = 2 * RAD + 1
    lanes = lanes_wide.shape[0]
    padded_cols = tile_cols + 2 * edge
    window_rows = tile_rows + 2 * RAD
    pixels_two = window_rows * width
    shift_row, shift_col, row_start, col_start = place[0], place[1], place[2], place[3]
    inv_root = channels ** (-0.5)

    across = lax.broadcasted_iota(jnp.int32, (padded_cols, channels), 0) + (col_start - edge)
    inside_cols = (across >= 0) & (across < image_cols)

    def masked(line, image_row):
        inside = inside_cols & (image_row >= 0) & (image_row < image_rows)
        return jnp.where(inside, line.astype(jnp.float32), 0.0)

    @pl.loop(0, tile_rows + 2)
    def _(line):
        cells = masked(pad_one[line], row_start - 1 + line)
        for tap in range(3):
            first = edge - 1 + tap
            taps_one[pl.ds(pl.multiple_of(line * tile_cols, 16), tile_cols),
                     tap * channels : (tap + 1) * channels] = (
                cells[first : first + tile_cols].astype(jnp.bfloat16)
            )

    @pl.loop(0, window_rows + 2)
    def _(line):
        at = shift_row + MAXOFF + line
        cells = masked(pad_two[at], row_start - (MAXOFF + RAD + 1) + at)
        cells = pltpu.roll(cells, padded_cols - (shift_col + edge - RAD - 1), 0)
        for tap in range(3):
            taps_two[pl.ds(pl.multiple_of(line * width, 16), width),
                     tap * channels : (tap + 1) * channels] = (
                cells[tap : tap + width].astype(jnp.bfloat16)
            )

    def convolved(taps, first, size, pitch):
        total = jnp.broadcast_to(bias[...], (size, channels))
        for tap in range(3):
            total = total + jnp.dot(
                taps[pl.ds(pl.multiple_of(first + tap * pitch, 16), size), :],
                weight[tap],
                preferred_element_type=jnp.float32,
            )
        return total

    group = 4
    size_one = group * tile_cols

    @pl.loop(0, tile_rows // group)
    def _(block):
        first = pl.multiple_of(block * size_one, 16)
        pre = convolved(taps_one, first, size_one, tile_cols)
        pre_one[pl.ds(first, size_one), :] = pre
        feat_one[pl.ds(first, size_one), :] = jnp.maximum(pre, 0.0).astype(jnp.bfloat16)

    size_two = group * width

    @pl.loop(0, window_rows // group)
    def _(block):
        first = pl.multiple_of(block * size_two, 16)
        pre = convolved(taps_two, first, size_two, width).reshape(group, width, channels)
        rows = lax.broadcasted_iota(jnp.int32, pre.shape, 0) + (
            row_start + shift_row - RAD + block * group
        )
        cols = lax.broadcasted_iota(jnp.int32, pre.shape, 1) + (col_start + shift_col - RAD)
        inside = (rows >= 0) & (rows < image_rows) & (cols >= 0) & (cols < image_cols)
        pre = jnp.where(inside, pre, 0.0).reshape(size_two, channels)
        pre_two[pl.ds(first, size_two), :] = pre
        feat_two[pl.ds(first, size_two), :] = jnp.maximum(pre, 0.0).astype(jnp.bfloat16)

    feat_two[pixels_two:, :] = jnp.zeros_like(feat_two[pixels_two:, :])
    grad_two[...] = jnp.zeros_like(grad_two)
    cot_wide[...] = cot[...].astype(jnp.float32)
    lanes_wide[...] = jnp.zeros_like(lanes_wide)

    def skew(cells, back):
        line = lax.rem(lax.broadcasted_iota(jnp.int32, cells.shape, 0), tile_cols)
        step = 1
        while step < tile_cols:
            moved = pltpu.roll(cells, lanes - step if back else step, 1)
            cells = jnp.where((line // step) % 2 == 1, moved, cells)
            step *= 2
        return cells

    @pl.loop(0, tile_rows // group)
    def _(block):
        at = pl.ds(pl.multiple_of(block * size_one, 128), size_one)
        for line in range(side):
            lanes_wide[line * width : line * width + side, :] = cot_wide[
                line * side : (line + 1) * side, at
            ]
        spread_all = skew(lanes_wide[...].T, False).astype(jnp.bfloat16)
        score_list = []
        for inner in range(group):
            row = block * group + inner
            spread = spread_all[inner * tile_cols : (inner + 1) * tile_cols]
            pixels = pl.ds(pl.multiple_of(row * tile_cols, 16), tile_cols)
            window = pl.ds(pl.multiple_of(row * width, 16), lanes)
            one, two = feat_one[pixels, :], feat_two[window, :]
            score_list.append(
                lax.dot_general(one, two, (((1,), (1,)), ((), ())), preferred_element_type=jnp.float32)
            )
            grad = jnp.dot(spread, two, preferred_element_type=jnp.float32) * inv_root
            grad = jnp.where(pre_one[pixels, :] > 0, grad, 0.0)
            delta_one[pixels, :] = grad.astype(jnp.bfloat16).astype(jnp.float32)
            grad_two[window, :] += lax.dot_general(
                spread, one, (((0,), (0,)), ((), ())), preferred_element_type=jnp.float32
            )
        scores = skew(jnp.concatenate(score_list, axis=0), True).T * inv_root
        for line in range(side):
            corr_wide[line * side : (line + 1) * side, at] = scores[
                line * width : line * width + side
            ]

    corr[...] = corr_wide[...].astype(jnp.bfloat16)
    delta_two = jnp.where(pre_two[...] > 0, grad_two[:pixels_two, :] * inv_root, 0.0)
    bias_term = jnp.sum(delta_one[...], axis=0, keepdims=True)
    bias_term = bias_term + jnp.sum(delta_two, axis=0, keepdims=True)
    flip_one[...] = delta_one[...].T.astype(jnp.bfloat16)
    flip_two[...] = delta_two.T.astype(jnp.bfloat16)

    half = channels // 2
    pixels_one = tile_rows * tile_cols
    for tap_row in range(3):
        for tap_col in range(3):
            cols = slice(tap_col * channels, (tap_col + 1) * channels)
            first_one, first_two = tap_row * tile_cols, tap_row * width
            term = jnp.dot(
                flip_one[...],
                taps_one[first_one : first_one + pixels_one, cols],
                preferred_element_type=jnp.float32,
            ) + jnp.dot(
                flip_two[...],
                taps_two[first_two : first_two + pixels_two, cols],
                preferred_element_type=jnp.float32,
            )
            term = term.T
            first = (tap_row * 3 + tap_col) * channels
            terms[0, first : first + channels, :] = term[:, :half]
            terms[1, first : first + channels, :] = term[:, half:]
    last = 9 * channels
    rest = terms.shape[1] - last
    filler = lax.broadcasted_iota(jnp.int32, (rest, channels), 0) == 0
    filler = jnp.where(filler, jnp.broadcast_to(bias_term, (rest, channels)), 0.0)
    terms[0, last:, :] = filler[:, :half]
    terms[1, last:, :] = filler[:, half:]


def spread_kernel(summed, grad_weight, grad_bias):
    rows, half = grad_weight.shape[0], summed.shape[2]
    for part in range(2):
        lanes = slice(part * half, (part + 1) * half)
        grad_weight[:, lanes] = summed[part, :rows, :].astype(jnp.float32)
        grad_bias[:, lanes] = summed[part, rows : rows + 16, :].astype(jnp.float32)[:1]


def shards(frames, offsets, weight, bias, cotangent):
    tile_rows, tile_cols, channels = (frames.shape[2], frames.shape[3], frames.shape[4])
    row_start = lax.axis_index("row") * tile_rows
    col_start = lax.axis_index("col") * tile_cols
    image_rows = lax.axis_size("row") * tile_rows
    image_cols = lax.axis_size("col") * tile_cols
    wide = MAXOFF + RAD + 1
    edge = (wide + 15) // 16 * 16
    side = 2 * RAD + 1
    width = (tile_cols + 2 * RAD + 15) // 16 * 16
    lanes = (side * width + 127) // 128 * 128
    window_rows = tile_rows + 2 * RAD
    pixels_one, pixels_two = tile_rows * tile_cols, window_rows * width
    long = max(pixels_two, (tile_rows - 1) * width + lanes)
    shift = offsets[0, row_start // BLK, col_start // BLK]
    place = jnp.concatenate([shift, jnp.stack([row_start, col_start])]).astype(jnp.int32)
    pad_one, pad_two = gather_halos(frames[0], wide, edge)
    whole = pl.BlockSpec(memory_space=pltpu.VMEM)
    rows = padded_rows(9 * channels + 1)
    geometry = (tile_rows, tile_cols, image_rows, image_cols, edge, width)
    corr, terms = pl.pallas_call(
        functools.partial(tile_kernel, geometry),
        out_shape=[
            jax.ShapeDtypeStruct((side * side, pixels_one), jnp.bfloat16),
            jax.ShapeDtypeStruct((2, rows, channels // 2), jnp.float32),
        ],
        in_specs=[pl.BlockSpec(memory_space=pltpu.SMEM)] + [whole] * 5,
        out_specs=[whole] * 2,
        scratch_shapes=[
            pltpu.VMEM(((tile_rows + 2) * tile_cols, 3 * channels), jnp.bfloat16),
            pltpu.VMEM(((window_rows + 2) * width, 3 * channels), jnp.bfloat16),
            pltpu.VMEM((pixels_one, channels), jnp.float32),
            pltpu.VMEM((pixels_two, channels), jnp.float32),
            pltpu.VMEM((pixels_one, channels), jnp.bfloat16),
            pltpu.VMEM((long, channels), jnp.bfloat16),
            pltpu.VMEM((pixels_one, channels), jnp.float32),
            pltpu.VMEM((channels, pixels_one), jnp.bfloat16),
            pltpu.VMEM((channels, pixels_two), jnp.bfloat16),
            pltpu.VMEM((long, channels), jnp.float32),
            pltpu.VMEM((side * side, pixels_one), jnp.float32),
            pltpu.VMEM((side * side, pixels_one), jnp.float32),
            pltpu.VMEM((lanes, 4 * tile_cols), jnp.float32),
        ],
        compiler_params=pltpu.CompilerParams(vmem_limit_bytes=48 * 2**20),
        name="tile_terms",
    )(
        place, pad_one, pad_two, weight.reshape(3, 3 * channels, channels), bias[None],
        cotangent[0].reshape(side * side, pixels_one),
    )
    summed = sum_everywhere(terms)
    grad_weight, grad_bias = pl.pallas_call(
        spread_kernel,
        out_shape=[
            jax.ShapeDtypeStruct((9 * channels, channels), jnp.float32),
            jax.ShapeDtypeStruct((1, channels), jnp.float32),
        ],
        in_specs=[whole],
        out_specs=[whole] * 2,
        compiler_params=pltpu.CompilerParams(vmem_limit_bytes=32 * 2**20),
        name="spread_sum",
    )(summed)
    return (
        corr.reshape(1, side * side, tile_rows, tile_cols),
        grad_weight.reshape(weight.shape),
        grad_bias[0],
    )


def solution(mesh):
    return jax.shard_map(
        shards,
        mesh=mesh,
        in_specs=(
            P("pair", None, "row", "col", None),
            P("pair", None, None, None),
            P(),
            P(),
            P("pair", None, "row", "col"),
        ),
        out_specs=(P("pair", None, "row", "col"), P(), P()),
        check_vma=False,
    )
```

time: 150 us -> 85.1 us (0.57)
  Pallas kernels: 39.1 us -> 77.2 us
  starting transfers between devices: 30.5 us -> 0 us
  local copies, waits for them, and re-layouts: 33.1 us -> 6.79 us
  matrix products: 18.5 us -> 0 us
  waiting for transfers between devices: 16.6 us -> 0 us
  other arithmetic: 6.6 us -> 0.08 us
  between operations: 4.95 us -> 0.71 us
    pallas_call x0 -> x3, Pallas kernels: none -> 36.9 us  [the longest x1 17.9 us: shards(): pl.pallas_call(functools.partial(tile_kernel, geometry), out_shape=[jax.S...]
    ppermute x12 -> x0, starting transfers between devices: 30.5 us -> none  [the longest x6 22.5 us: with_halo(): lax.ppermute(tail, axis, [(i, (i + 1) % count) for i in range(ends)])]
    dot_general x63 -> x0, matrix products: 18.5 us -> none  [the longest x18 4.89 us: convolve(): jnp.dot(window, weight[tap_row, tap_col], preferred_element_type=jnp.floa...]
    ppermute x12 -> x0, waiting for transfers between devices: 16.6 us -> none  [the longest x6 12.8 us: with_halo(): lax.ppermute(head, axis, [((i + 1) % count, i) for i in range(ends)])]
    dynamic_update_slice x1 -> x0, local copies, waits for them, and re-layouts: 9.61 us -> none  [shards(): lax.dynamic_update_slice(gradient_second_padded, grad_window * inv_root,...]
    reshape x36 -> x0, local copies, waits for them, and re-layouts: 9.03 us -> none  [the longest x9 3.12 us: band_spread(): flattened.reshape(row_count, col_count, patch_width + 1)[:, :, :patch_width]]
    concatenate x6 -> x1, other arithmetic: 4.17 us -> 0.08 us  [shards(): jnp.concatenate([shift, jnp.stack([row_start, col_start])])]
    slice x10 -> x0, local copies, waits for them, and re-layouts: 3.38 us -> none  [the longest x1 1.61 us: convolve(): padded[tap_row:tap_row + row_count, tap_col:tap_col + col_count]]
  transfers between devices with their start and end apart: 12 -> 0, of which waited for: 6 -> 0; matrix products, arithmetic and copies ran while one was open for 9% -> 0% of each run, Pallas kernels for 0% -> 0%
where the time goes in v2:
time: 85.1 us; the launch traced here: 84.8 us
  Pallas kernels  77.2 us (91%)
  local copies, waits for them, and re-layouts  6.79 us (8%)
    pallas_call x1, Pallas kernels, sum_everywhere(): pl.pallas_call(functools.partial(sum_kernel, plans), out_shape=jax.ShapeD...  40.3 us
    pallas_call x1, Pallas kernels, shards(): pl.pallas_call(functools.partial(tile_kernel, geometry), out_shape=[jax.S...  17.9 us
    pallas_call x1, Pallas kernels, gather_halos(): pl.pallas_call(functools.partial(halo_kernel, wide, edge), out_shape=pads...  17.4 us
    unnamed x10, local copies, waits for them, and re-layouts  4.99 us

profile of v2, /device:TPU:0, one launch (start us, length us, event | category | flops | bytes accessed | tf_op | source)
XLA Modules:
  0.0 84.8 jit_solution(2957647893585852974)
XLA Ops:
  0.6 0.0 copy-start
  0.7 0.6 copy-done
  1.3 0.1 pad_add_fusion.place
  1.4 1.0 %copy.10.cot = bf16[81,512]{1,0:T(8,128)(2,1)S(1)} copy(bf16[81,512]{0,1:T(8,128)(2,1)} %bitcast.14) | data formatting | bytes 165888 | tf_op jit(solution)/shard_map/reshape;squeeze | solution.py:444
  2.4 17.4 %gather_halos.1 = (bf16[18,64,256]{2,1,0:T(8,128)(2,1)}, bf16[42,64,256]{2,1,0:T(8,128)(2,1)}) custom-call(bf16[2,16,32,256]{3,2,1,0:T(8,128)(2,1)} %bitcast.13), custom_call_target="tpu_custom_call" | custom-call | tf_op jit(solution)/shard_map/gather_halos/pallas_call | solution.py:218
  19.8 0.0 copy-start.1
  19.8 1.3 %copy-done.1 = bf16[42,64,256]{2,1,0:T(8,128)(2,1)S(1)} copy-done((bf16[42,64,256]{2,1,0:T(8,128)(2,1)S(1)}, bf16[42,64,256]{2,1,0:T(8,128)(2,1)}, u32[]{:S(2)}) %copy-start.1) | copy-done | bytes 1376280
  21.2 0.0 copy-start.2
  21.2 1.3 %copy-done.2 = bf16[3,3,256,256]{3,2,1,0:T(8,128)(2,1)S(1)} copy-done((bf16[3,3,256,256]{3,2,1,0:T(8,128)(2,1)S(1)}, bf16[3,3,256,256]{3,2,1,0:T(8,128)(2,1)}, u32[]{:S(2)}) %copy-start.2) | copy-done | bytes 1179672
  22.4 0.0 copy-start.3
  22.4 1.1 %copy-done.3 = bf16[18,64,256]{2,1,0:T(8,128)(2,1)S(1)} copy-done((bf16[18,64,256]{2,1,0:T(8,128)(2,1)S(1)}, bf16[18,64,256]{2,1,0:T(8,128)(2,1)}, u32[]{:S(2)}) %copy-start.3) | copy-done | bytes 589848
  23.5 0.0 copy-start.4
  23.5 0.7 copy-done.4
  24.2 17.9 %tile_terms.1 = (bf16[81,512]{1,0:T(8,128)(2,1)S(1)}, f32[2,2560,128]{2,1,0:T(8,128)S(1)}) custom-call(s32[4]{0:T(128)S(1)} %pad_add_fusion.place, bf16[18,64,256]{2,1,0:T(8,128)(2,1)S(1)} %copy-done.3, bf16[42,64,256]{2,1,0:T(8,128)(2,1)S(1)} %copy-done.1, bf16[3,768,256]{2,1,0:T(8,128)(2,1)S(1)} %bitcast.11, f32[1,256]{1,0:T(1,128)S(1)} %bitcast.12, ...), custom_call_target="tpu_custom_call" | custom-call | tf_op jit(solution)/shard_map/tile_terms/pallas_call | solution.py:417
  42.1 0.8 copy.11
  42.9 40.3 %sum_everywhere.1.summed = bf16[2,2560,128]{2,1,0:T(8,128)(2,1)S(1)} custom-call(f32[2,2560,128]{2,1,0:T(8,128)S(1)} %get-tuple-element.12.terms), custom_call_target="tpu_custom_call" | custom-call | tf_op jit(solution)/shard_map/sum_everywhere/pallas_call | solution.py:133
  83.2 1.6 %spread_sum.1 = (f32[2304,256]{1,0:T(8,128)}, f32[1,256]{1,0:T(1,128)}) custom-call(bf16[2,2560,128]{2,1,0:T(8,128)(2,1)S(1)} %sum_everywhere.1.summed), custom_call_target="tpu_custom_call" | custom-call | tf_op jit(solution)/shard_map/spread_sum/pallas_call | solution.py:447
  (1 shorter events, 0.0 us)
Async XLA Ops:
  0.6 0.7 copy-start
  19.8 1.3 %copy-start.1 = (bf16[42,64,256]{2,1,0:T(8,128)(2,1)S(1)}, bf16[42,64,256]{2,1,0:T(8,128)(2,1)}, u32[]{:S(2)}) copy-start(bf16[42,64,256]{2,1,0:T(8,128)(2,1)} %get-tuple-element.10.pad_two) | copy-start | bytes 4128772
  21.2 1.3 %copy-start.2 = (bf16[3,3,256,256]{3,2,1,0:T(8,128)(2,1)S(1)}, bf16[3,3,256,256]{3,2,1,0:T(8,128)(2,1)}, u32[]{:S(2)}) copy-start(bf16[3,3,256,256]{3,2,1,0:T(8,128)(2,1)} %param.7) | copy-start | bytes 3538948
  22.4 1.1 %copy-start.3 = (bf16[18,64,256]{2,1,0:T(8,128)(2,1)S(1)}, bf16[18,64,256]{2,1,0:T(8,128)(2,1)}, u32[]{:S(2)}) copy-start(bf16[18,64,256]{2,1,0:T(8,128)(2,1)} %get-tuple-element.9.pad_one) | copy-start | bytes 1769476
  23.5 0.7 copy-start.4

commit v3 on v2

--- a/solution.py
+++ b/solution.py
@@ -14,7 +14,7 @@
 
 
 def exchange_plan():
-    sizes = {axis: lax.axis_size(axis) for axis in ("row", "col", "pair")}
+    sizes = {axis: lax.axis_size(axis) for axis in ("row", "col")}
     bits = {
         axis: [1 << place for place in range(size.bit_length() - 1)]
         for axis, size in sizes.items()
@@ -22,99 +22,141 @@
     near = [("row", stride) for stride in bits["row"][:1]]
     rest = [("row", stride) for stride in bits["row"][1:]]
     side = [("col", stride) for stride in reversed(bits["col"])]
-    deep = [("pair", stride) for stride in reversed(bits["pair"])]
-    return [near + rest + side + deep, near + side + rest + deep]
-
-
-def sum_kernel(plans, terms, total, acc, send_half, recv_half, recv_wide, *sems):
-    rs_send, rs_recv, ag_send, ag_recv = sems
-    rows = terms.shape[1]
+    return [near + rest + side, near + side + rest]
+
+
+def sum_kernel(plans, runs, terms, total, acc, send_half, recv_half, recv_wide, *sems):
+    rs_send, rs_recv, ag_send, ag_recv, far_send, far_recv = sems
     count = len(plans[0])
-    parts = range(len(plans))
+    parts = range(len(runs))
+    depth = lax.axis_size("pair")
+    me = lax.axis_index("pair")
 
     def partner(step):
         axis, stride = step
-        me = lax.axis_index(axis)
-        bit = lax.rem(me // stride, 2)
-        return bit, {axis: me + stride - 2 * stride * bit}
+        at = lax.axis_index(axis)
+        bit = lax.rem(at // stride, 2)
+        return bit, {axis: at + stride - 2 * stride * bit}
+
+    def peer(hop):
+        return lax.rem(me + hop, depth)
 
     barrier = pltpu.get_barrier_semaphore()
     for step in plans[0]:
         pl.semaphore_signal(barrier, inc=1, device_id=partner(step)[1], device_id_type=MESH)
-    pl.semaphore_wait(barrier, count)
-
-    base = [0 for _ in parts]
+    for hop in range(1, depth):
+        pl.semaphore_signal(barrier, inc=1, device_id={"pair": peer(hop)}, device_id_type=MESH)
+    pl.semaphore_wait(barrier, count + depth - 1)
+
+    base = [start for _, start, _ in runs]
     trail = [[] for _ in parts]
     waiting = [None for _ in parts]
     sent = []
 
+    def send(src, dst, send_sem, recv_sem, device):
+        copy = pltpu.make_async_remote_copy(
+            src_ref=src,
+            dst_ref=dst,
+            send_sem=send_sem,
+            recv_sem=recv_sem,
+            device_id=device,
+            device_id_type=MESH,
+        )
+        copy.start()
+        sent.append(copy)
+        return copy
+
     def absorb(part, place):
+        half, _, rows = runs[part]
         size = rows >> (place + 1)
-        copy, keep, came, wide = waiting[part]
+        copy, keep, came = waiting[part]
         copy.wait_recv()
         source = terms if place == 0 else acc
-        add = came[...] if wide else came[...].astype(jnp.float32)
-        acc[part, pl.ds(keep, size), :] = source[part, pl.ds(keep, size), :] + add
+        acc[half, pl.ds(keep, size), :] = source[half, pl.ds(keep, size), :] + came[...].astype(
+            jnp.float32
+        )
         base[part] = keep
 
     for place in range(count):
-        size = rows >> (place + 1)
-        slot = rows - (rows >> place)
-        wide = place == 0 or place == count - 1
         for part in parts:
+            half, start, rows = runs[part]
+            size = rows >> (place + 1)
+            slot = start + rows - (rows >> place)
             if place > 0:
                 absorb(part, place - 1)
-            bit, device = partner(plans[part][place])
+            bit, device = partner(plans[half][place])
             keep = pl.multiple_of(base[part] + bit * size, 16)
             give = pl.multiple_of(base[part] + (1 - bit) * size, 16)
-            if wide:
-                source = terms if place == 0 else acc
-                first = 0 if place == 0 else rows // 2
-                src = source.at[part, pl.ds(give, size), :]
-                dst = recv_wide.at[part, pl.ds(first, size), :]
+            if place == 0:
+                src = terms.at[half, pl.ds(give, size), :]
+                dst = recv_wide.at[half, pl.ds(start // 2, size), :]
             else:
-                send_half[part, slot : slot + size, :] = acc[part, pl.ds(give, size), :].astype(
+                send_half[half, slot : slot + size, :] = acc[half, pl.ds(give, size), :].astype(
                     jnp.bfloat16
                 )
-                src = send_half.at[part, pl.ds(slot, size), :]
-                dst = recv_half.at[part, pl.ds(slot, size), :]
-            copy = pltpu.make_async_remote_copy(
-                src_ref=src,
-                dst_ref=dst,
-                send_sem=rs_send.at[part, place],
-                recv_sem=rs_recv.at[part, place],
-                device_id=device,
-                device_id_type=MESH,
-            )
-            copy.start()
-            sent.append(copy)
-            waiting[part] = (copy, keep, dst, wide)
+                src = send_half.at[half, pl.ds(slot, size), :]
+                dst = recv_half.at[half, pl.ds(slot, size), :]
+            copy = send(src, dst, rs_send.at[part, place], rs_recv.at[part, place], device)
+            waiting[part] = (copy, keep, dst)
             trail[part].append(base[part])
+
+    arrivals = [[] for _ in parts]
     for part in parts:
+        half, start, rows = runs[part]
         absorb(part, count - 1)
-        size = rows >> count
-        own = pl.multiple_of(base[part], 16)
-        total[part, pl.ds(own, size), :] = acc[part, pl.ds(own, size), :].astype(jnp.bfloat16)
+        size = (rows >> count) // depth
+        slot = start + rows - (rows >> count)
+        for hop in range(1, depth):
+            give = pl.multiple_of(base[part] + peer(hop) * size, 16)
+            first = slot + (hop - 1) * size
+            send_half[half, first : first + size, :] = acc[half, pl.ds(give, size), :].astype(
+                jnp.bfloat16
+            )
+            src = send_half.at[half, pl.ds(first, size), :]
+            dst = recv_half.at[half, pl.ds(first, size), :]
+            copy = send(
+                src, dst, far_send.at[part, hop], far_recv.at[part, hop], {"pair": peer(hop)}
+            )
+            arrivals[part].append((copy, dst))
+    for part in parts:
+        half, start, rows = runs[part]
+        size = (rows >> count) // depth
+        own = pl.ds(pl.multiple_of(base[part] + me * size, 16), size)
+        value = acc[half, own, :]
+        for copy, came in arrivals[part]:
+            copy.wait_recv()
+            value = value + came[...].astype(jnp.float32)
+        total[half, own, :] = value.astype(jnp.bfloat16)
+        block = total.at[half, own, :]
+        arrivals[part] = [
+            send(
+                block,
+                block,
+                far_send.at[part, depth - 1 + hop],
+                far_recv.at[part, depth - 1 + hop],
+                {"pair": peer(hop)},
+            )
+            for hop in range(1, depth)
+        ]
     for place in reversed(range(count)):
-        size = rows >> (place + 1)
         for part in parts:
-            if place < count - 1:
-                waiting[part].wait_recv()
-            block = total.at[part, pl.ds(pl.multiple_of(base[part], 16), size), :]
-            copy = pltpu.make_async_remote_copy(
-                src_ref=block,
-                dst_ref=block,
-                send_sem=ag_send.at[part, place],
-                recv_sem=ag_recv.at[part, place],
-                device_id=partner(plans[part][place])[1],
-                device_id_type=MESH,
-            )
-            copy.start()
-            sent.append(copy)
-            waiting[part] = copy
+            half, start, rows = runs[part]
+            size = rows >> (place + 1)
+            for copy in arrivals[part]:
+                copy.wait_recv()
+            block = total.at[half, pl.ds(pl.multiple_of(base[part], 16), size), :]
+            copy = send(
+                block,
+                block,
+                ag_send.at[part, place],
+                ag_recv.at[part, place],
+                partner(plans[half][place])[1],
+            )
+            arrivals[part] = [copy]
             base[part] = trail[part][place]
     for part in parts:
-        waiting[part].wait_recv()
+        for copy in arrivals[part]:
+            copy.wait_recv()
     for copy in sent:
         copy.wait_send()
 
@@ -127,11 +169,16 @@
 
 def sum_everywhere(terms):
     plans = exchange_plan()
-    parts, rows, lanes = terms.shape
-    count = len(plans[0])
-    semaphores = pltpu.SemaphoreType.DMA((parts, count))
+    rows = terms.shape[1]
+    grains = rows // padded_rows(1)
+    head = (grains + 1) // 2 * padded_rows(1)
+    runs = [(half, 0, head) for half in range(2)]
+    if head < rows:
+        runs += [(half, head, rows - head) for half in range(2)]
+    near = pltpu.SemaphoreType.DMA((len(runs), len(plans[0])))
+    far = pltpu.SemaphoreType.DMA((len(runs), 2 * lax.axis_size("pair")))
     return pl.pallas_call(
-        functools.partial(sum_kernel, plans),
+        functools.partial(sum_kernel, plans, runs),
         out_shape=jax.ShapeDtypeStruct(terms.shape, jnp.bfloat16),
         in_specs=[pl.BlockSpec(memory_space=pltpu.VMEM)],
         out_specs=pl.BlockSpec(memory_space=pltpu.VMEM),
@@ -140,10 +187,12 @@
             pltpu.VMEM(terms.shape, jnp.bfloat16),
             pltpu.VMEM(terms.shape, jnp.bfloat16),
             pltpu.VMEM(terms.shape, jnp.float32),
-            semaphores,
-            semaphores,
-            semaphores,
-            semaphores,
+            near,
+            near,
+            near,
+            near,
+            far,
+            far,
         ],
         compiler_params=pltpu.CompilerParams(
             collective_id=1, has_side_effects=True, vmem_limit_bytes=32 * 2**20
@@ -152,7 +201,9 @@
     )(terms)
 
 
-def halo_kernel(wide, edge, frames, pad_one, pad_two, send_sem, recv_sem, own_sem):
+def halo_kernel(
+    wide, edge, frames, pad_one, pad_two, sides, cells, send_sem, recv_sem, own_sem
+):
     row, col = lax.axis_index("row"), lax.axis_index("col")
     row_count, col_count = lax.axis_size("row"), lax.axis_size("col")
     tile_rows, tile_cols = frames.shape[1], frames.shape[2]
@@ -178,6 +229,10 @@
         @pl.when(lies(*way))
         def _():
             pl.semaphore_signal(barrier, inc=1, device_id=device(*way), device_id_type=MESH)
+    first = frames[0, :, :edge, :].astype(jnp.float32)
+    cells[0] = first[:, 0, :].astype(jnp.bfloat16)
+    final = frames[0, :, tile_cols - edge :, :].astype(jnp.float32)
+    cells[1] = final[:, edge - 1, :].astype(jnp.bfloat16)
     own = []
     for frame, (pad, halo) in enumerate(((pad_one, 1), (pad_two, wide))):
         middle = pad.at[pl.ds(halo, tile_rows), pl.ds(edge, tile_cols), :]
@@ -191,9 +246,14 @@
         for frame, (pad, halo) in enumerate(((pad_one, 1), (pad_two, wide))):
             take_rows, put_rows = span(way[0], tile_rows, halo)
             take_cols, put_cols = span(way[1], tile_cols, edge)
+            source = frames.at[frame, take_rows, take_cols, :]
+            target = pad.at[put_rows, put_cols, :]
+            if frame == 0 and way[0] == 0:
+                source = cells.at[1 if way[1] > 0 else 0]
+                target = sides.at[0 if way[1] > 0 else 1]
             copy = pltpu.make_async_remote_copy(
-                src_ref=frames.at[frame, take_rows, take_cols, :],
-                dst_ref=pad.at[put_rows, put_cols, :],
+                src_ref=source,
+                dst_ref=target,
                 send_sem=send_sem.at[place, frame],
                 recv_sem=recv_sem.at[place, frame],
                 device_id=device(*way),
@@ -215,25 +275,30 @@
         jax.ShapeDtypeStruct((tile_rows + 2 * halo, tile_cols + 2 * edge, channels), frames.dtype)
         for halo in (1, wide)
     ]
+    pads.append(jax.ShapeDtypeStruct((2, tile_rows, channels), frames.dtype))
+    whole = pl.BlockSpec(memory_space=pltpu.VMEM)
     return pl.pallas_call(
         functools.partial(halo_kernel, wide, edge),
         out_shape=pads,
-        in_specs=[pl.BlockSpec(memory_space=pl.ANY)],
-        out_specs=[pl.BlockSpec(memory_space=pl.ANY)] * 2,
+        in_specs=[whole],
+        out_specs=[whole] * 3,
         scratch_shapes=[
+            pltpu.VMEM((2, tile_rows, channels), frames.dtype),
             pltpu.SemaphoreType.DMA((8, 2)),
             pltpu.SemaphoreType.DMA((8, 2)),
             pltpu.SemaphoreType.DMA((2,)),
         ],
-        compiler_params=pltpu.CompilerParams(collective_id=0, has_side_effects=True),
+        compiler_params=pltpu.CompilerParams(
+            collective_id=0, has_side_effects=True, vmem_limit_bytes=16 * 2**20
+        ),
         name="gather_halos",
     )(frames)
 
 
 def tile_kernel(
-    geometry, place, pad_one, pad_two, weight, bias, cot, corr, terms,
+    geometry, place, pad_one, pad_two, sides, weight, bias, cot, corr, terms,
     taps_one, taps_two, pre_one, pre_two, feat_one, feat_two, delta_one, flip_one, flip_two,
-    grad_two, cot_wide, corr_wide, lanes_wide,
+    grad_two, cot_wide, corr_wide, lanes_wide, sides_wide,
 ):
     tile_rows, tile_cols, image_rows, image_cols, edge, width = geometry
     channels = bias.shape[1]
@@ -252,9 +317,19 @@
         inside = inside_cols & (image_row >= 0) & (image_row < image_rows)
         return jnp.where(inside, line.astype(jnp.float32), 0.0)
 
+    sides_wide[:, :8, :] = jnp.zeros_like(sides_wide[:, :8, :])
+    sides_wide[:, 8 : 8 + tile_rows, :] = sides[...].astype(jnp.float32)
+    sides_wide[:, 8 + tile_rows :, :] = jnp.zeros_like(sides_wide[:, 8 + tile_rows :, :])
+    spot = across - (col_start - edge)
+
     @pl.loop(0, tile_rows + 2)
     def _(line):
-        cells = masked(pad_one[line], row_start - 1 + line)
+        cells = pad_one[line].astype(jnp.float32)
+        middle = (line > 0) & (line < tile_rows + 1)
+        for end, column in enumerate((edge - 1, edge + tile_cols)):
+            side_line = sides_wide[end, pl.ds(line + 7, 1), :]
+            cells = jnp.where((spot == column) & middle, side_line, cells)
+        cells = masked(cells, row_start - 1 + line)
         for tap in range(3):
             first = edge - 1 + tap
             taps_one[pl.ds(pl.multiple_of(line * tile_cols, 16), tile_cols),
@@ -410,7 +485,7 @@
     long = max(pixels_two, (tile_rows - 1) * width + lanes)
     shift = offsets[0, row_start // BLK, col_start // BLK]
     place = jnp.concatenate([shift, jnp.stack([row_start, col_start])]).astype(jnp.int32)
-    pad_one, pad_two = gather_halos(frames[0], wide, edge)
+    pad_one, pad_two, sides = gather_halos(frames[0], wide, edge)
     whole = pl.BlockSpec(memory_space=pltpu.VMEM)
     rows = padded_rows(9 * channels + 1)
     geometry = (tile_rows, tile_cols, image_rows, image_cols, edge, width)
@@ -420,7 +495,7 @@
             jax.ShapeDtypeStruct((side * side, pixels_one), jnp.bfloat16),
             jax.ShapeDtypeStruct((2, rows, channels // 2), jnp.float32),
         ],
-        in_specs=[pl.BlockSpec(memory_space=pltpu.SMEM)] + [whole] * 5,
+        in_specs=[pl.BlockSpec(memory_space=pltpu.SMEM)] + [whole] * 6,
         out_specs=[whole] * 2,
         scratch_shapes=[
             pltpu.VMEM(((tile_rows + 2) * tile_cols, 3 * channels), jnp.bfloat16),
@@ -436,11 +511,12 @@
             pltpu.VMEM((side * side, pixels_one), jnp.float32),
             pltpu.VMEM((side * side, pixels_one), jnp.float32),
             pltpu.VMEM((lanes, 4 * tile_cols), jnp.float32),
+            pltpu.VMEM((2, tile_rows + 16, channels), jnp.float32),
         ],
         compiler_params=pltpu.CompilerParams(vmem_limit_bytes=48 * 2**20),
         name="tile_terms",
     )(
-        place, pad_one, pad_two, weight.reshape(3, 3 * channels, channels), bias[None],
+        place, pad_one, pad_two, sides, weight.reshape(3, 3 * channels, channels), bias[None],
         cotangent[0].reshape(side * side, pixels_one),
     )
     summed = sum_everywhere(terms)

time: 85.1 us -> 69 us (0.81)
  Pallas kernels: 77.2 us -> 62.5 us
  local copies, waits for them, and re-layouts: 6.79 us -> 5.44 us
    pallas_call x1, Pallas kernels: 40.3 us -> 31.3 us  [sum_everywhere(): pl.pallas_call(functools.partial(sum_kernel, plans, runs), out_shape=jax....]
    pallas_call x1, Pallas kernels: 17.4 us -> 11.6 us  [gather_halos(): pl.pallas_call(functools.partial(halo_kernel, wide, edge), out_shape=pads...]
    unnamed x10 -> x8, local copies, waits for them, and re-layouts: 4.99 us -> 3.63 us
where the time goes in v3:
time: 69 us; the launch traced here: 68.7 us
  Pallas kernels  62.5 us (91%)
  local copies, waits for them, and re-layouts  5.44 us (8%)
  between operations  0.71 us (1%)
    pallas_call x1, Pallas kernels, sum_everywhere(): pl.pallas_call(functools.partial(sum_kernel, plans, runs), out_shape=jax....  31.3 us
    pallas_call x1, Pallas kernels, shards(): pl.pallas_call(functools.partial(tile_kernel, geometry), out_shape=[jax.S...  18 us
    pallas_call x1, Pallas kernels, gather_halos(): pl.pallas_call(functools.partial(halo_kernel, wide, edge), out_shape=pads...  11.6 us
    unnamed x8, local copies, waits for them, and re-layouts  3.63 us
    pallas_call x1, Pallas kernels, shards(): pl.pallas_call(spread_kernel, out_shape=[jax.ShapeDtypeStruct((9 * channe...  1.58 us

profile of v3, /device:TPU:0, one launch (start us, length us, event | category | flops | bytes accessed | tf_op | source)
XLA Modules:
  0.0 68.7 jit_solution(14517872463105283144)
XLA Ops:
  0.6 0.0 copy-start
  0.7 0.6 copy-done
  1.3 0.1 pad_add_fusion.place
  1.4 1.0 %copy.10.cot = bf16[81,512]{1,0:T(8,128)(2,1)S(1)} copy(bf16[81,512]{0,1:T(8,128)(2,1)} %bitcast.14) | data formatting | bytes 165888 | tf_op jit(solution)/shard_map/reshape;squeeze | solution.py:520
  2.4 0.0 copy-start.2
  2.4 1.0 %copy-done.2 = bf16[1,2,16,32,256]{4,3,2,1,0:T(8,128)(2,1)S(1)} copy-done((bf16[1,2,16,32,256]{4,3,2,1,0:T(8,128)(2,1)S(1)}, bf16[1,2,16,32,256]{4,3,2,1,0:T(8,128)(2,1)}, u32[]{:S(2)}) %copy-start.2) | copy-done | bytes 524312
  3.5 11.6 %gather_halos.1 = (bf16[18,64,256]{2,1,0:T(8,128)(2,1)S(1)}, bf16[42,64,256]{2,1,0:T(8,128)(2,1)S(1)}, bf16[2,16,256]{2,1,0:T(8,128)(2,1)S(1)}) custom-call(bf16[2,16,32,256]{3,2,1,0:T(8,128)(2,1)S(1)} %bitcast.12), custom_call_target="tpu_custom_call" | custom-call | tf_op jit(solution)/shard_map/gather_halos/pallas_call | solution.py:280
  15.1 0.0 copy-start.1
  15.1 1.3 %copy-done.1 = bf16[3,3,256,256]{3,2,1,0:T(8,128)(2,1)S(1)} copy-done((bf16[3,3,256,256]{3,2,1,0:T(8,128)(2,1)S(1)}, bf16[3,3,256,256]{3,2,1,0:T(8,128)(2,1)}, u32[]{:S(2)}) %copy-start.1) | copy-done | bytes 1179672
  16.3 0.0 copy-start.3
  16.3 0.7 copy-done.3
  17.0 18.0 %tile_terms.1 = (bf16[81,512]{1,0:T(8,128)(2,1)S(1)}, f32[2,2560,128]{2,1,0:T(8,128)S(1)}) custom-call(s32[4]{0:T(128)S(1)} %pad_add_fusion.place, bf16[18,64,256]{2,1,0:T(8,128)(2,1)S(1)} %get-tuple-element.10.pad_one, bf16[42,64,256]{2,1,0:T(8,128)(2,1)S(1)} %get-tuple-element.11.pad_two, bf16[2,16,256]{2,1,0:T(8,128)(2,1)S(1)} %get-tuple-element.12.sides, ...), custom_call_target="tpu_custom_call" | custom-call | tf_op jit(solution)/shard_map/tile_terms/pallas_call | solution.py:492
  35.1 0.8 %copy.11 = bf16[81,512]{0,1:T(8,128)(2,1)} copy(bf16[81,512]{1,0:T(8,128)(2,1)S(1)} %get-tuple-element.13) | data formatting | bytes 165888 | tf_op jit(solution)/shard_map/tile_terms/pallas_call | solution.py:492
  35.8 31.3 %sum_everywhere.1.summed = bf16[2,2560,128]{2,1,0:T(8,128)(2,1)S(1)} custom-call(f32[2,2560,128]{2,1,0:T(8,128)S(1)} %get-tuple-element.14.terms), custom_call_target="tpu_custom_call" | custom-call | tf_op jit(solution)/shard_map/sum_everywhere/pallas_call | solution.py:180
  67.2 1.6 %spread_sum.1 = (f32[2304,256]{1,0:T(8,128)}, f32[1,256]{1,0:T(1,128)}) custom-call(bf16[2,2560,128]{2,1,0:T(8,128)(2,1)S(1)} %sum_everywhere.1.summed), custom_call_target="tpu_custom_call" | custom-call | tf_op jit(solution)/shard_map/spread_sum/pallas_call | solution.py:523
  (1 shorter events, 0.0 us)
Async XLA Ops:
  0.6 0.7 %copy-start = (s32[1,2,2,2]{3,2,1,0:T(2,128)S(1)}, s32[1,2,2,2]{3,2,1,0:T(2,128)}, u32[]{:S(2)}) copy-start(s32[1,2,2,2]{3,2,1,0:T(2,128)} %param.6) | copy-start | bytes 100
  2.4 1.0 %copy-start.2 = (bf16[1,2,16,32,256]{4,3,2,1,0:T(8,128)(2,1)S(1)}, bf16[1,2,16,32,256]{4,3,2,1,0:T(8,128)(2,1)}, u32[]{:S(2)}) copy-start(bf16[1,2,16,32,256]{4,3,2,1,0:T(8,128)(2,1)} %param.5) | copy-start | bytes 1572868
  15.1 1.3 %copy-start.1 = (bf16[3,3,256,256]{3,2,1,0:T(8,128)(2,1)S(1)}, bf16[3,3,256,256]{3,2,1,0:T(8,128)(2,1)}, u32[]{:S(2)}) copy-start(bf16[3,3,256,256]{3,2,1,0:T(8,128)(2,1)} %param.7) | copy-start | bytes 3538948
  16.3 0.7 copy-start.3

commit v4 on v3

--- a/solution.py
+++ b/solution.py
@@ -11,6 +11,17 @@
 RAD = 4
 MAXOFF = 8
 MESH = pl.DeviceIdType.MESH
+
+
+def skew(cells, period, back):
+    lanes = cells.shape[1]
+    line = lax.rem(lax.broadcasted_iota(jnp.int32, cells.shape, 0), period)
+    step = 1
+    while step < period:
+        moved = pltpu.roll(cells, lanes - step if back else step, 1)
+        cells = jnp.where((line // step) % 2 == 1, moved, cells)
+        step *= 2
+    return cells
 
 
 def exchange_plan():
@@ -25,7 +36,10 @@
     return [near + rest + side, near + side + rest]
 
 
-def sum_kernel(plans, runs, terms, total, acc, send_half, recv_half, recv_wide, *sems):
+def sum_kernel(
+    plans, runs, shape, terms, scores, total, corr,
+    acc, send_half, recv_half, recv_wide, corr_wide, *sems,
+):
     rs_send, rs_recv, ag_send, ag_recv, far_send, far_recv = sems
     count = len(plans[0])
     parts = range(len(runs))
@@ -47,6 +61,24 @@
     for hop in range(1, depth):
         pl.semaphore_signal(barrier, inc=1, device_id={"pair": peer(hop)}, device_id_type=MESH)
     pl.semaphore_wait(barrier, count + depth - 1)
+
+    tile_cols, width, group, inv_root = shape
+    side = 2 * RAD + 1
+    chunk = group * tile_cols
+    blocks = list(range(scores.shape[0] // chunk))
+
+    def take_band():
+        if not blocks:
+            return
+        at = slice(blocks[0] * chunk, (blocks[0] + 1) * chunk)
+        bands = skew(scores[at, :], tile_cols, True).T * inv_root
+        for line in range(side):
+            corr_wide[line * side : (line + 1) * side, at] = bands[
+                line * width : line * width + side
+            ]
+        blocks.pop(0)
+        if not blocks:
+            corr[...] = corr_wide[...].astype(jnp.bfloat16)
 
     base = [start for _, start, _ in runs]
     trail = [[] for _ in parts]
@@ -99,6 +131,7 @@
             copy = send(src, dst, rs_send.at[part, place], rs_recv.at[part, place], device)
             waiting[part] = (copy, keep, dst)
             trail[part].append(base[part])
+        take_band()
 
     arrivals = [[] for _ in parts]
     for part in parts:
@@ -118,6 +151,7 @@
                 src, dst, far_send.at[part, hop], far_recv.at[part, hop], {"pair": peer(hop)}
             )
             arrivals[part].append((copy, dst))
+    take_band()
     for part in parts:
         half, start, rows = runs[part]
         size = (rows >> count) // depth
@@ -154,6 +188,9 @@
             )
             arrivals[part] = [copy]
             base[part] = trail[part][place]
+        take_band()
+    while blocks:
+        take_band()
     for part in parts:
         for copy in arrivals[part]:
             copy.wait_recv()
@@ -167,7 +204,7 @@
     return (rows + grain - 1) // grain * grain
 
 
-def sum_everywhere(terms):
+def sum_everywhere(terms, scores, shape):
     plans = exchange_plan()
     rows = terms.shape[1]
     grains = rows // padded_rows(1)
@@ -178,15 +215,19 @@
     near = pltpu.SemaphoreType.DMA((len(runs), len(plans[0])))
     far = pltpu.SemaphoreType.DMA((len(runs), 2 * lax.axis_size("pair")))
     return pl.pallas_call(
-        functools.partial(sum_kernel, plans, runs),
-        out_shape=jax.ShapeDtypeStruct(terms.shape, jnp.bfloat16),
-        in_specs=[pl.BlockSpec(memory_space=pltpu.VMEM)],
-        out_specs=pl.BlockSpec(memory_space=pltpu.VMEM),
+        functools.partial(sum_kernel, plans, runs, shape),
+        out_shape=[
+            jax.ShapeDtypeStruct(terms.shape, jnp.bfloat16),
+            jax.ShapeDtypeStruct(((2 * RAD + 1) ** 2, scores.shape[0]), jnp.bfloat16),
+        ],
+        in_specs=[pl.BlockSpec(memory_space=pltpu.VMEM)] * 2,
+        out_specs=[pl.BlockSpec(memory_space=pltpu.VMEM)] * 2,
         scratch_shapes=[
             pltpu.VMEM(terms.shape, jnp.float32),
             pltpu.VMEM(terms.shape, jnp.bfloat16),
             pltpu.VMEM(terms.shape, jnp.bfloat16),
             pltpu.VMEM(terms.shape, jnp.float32),
+            pltpu.VMEM(((2 * RAD + 1) ** 2, scores.shape[0]), jnp.float32),
             near,
             near,
             near,
@@ -198,11 +239,12 @@
             collective_id=1, has_side_effects=True, vmem_limit_bytes=32 * 2**20
         ),
         name="sum_everywhere",
-    )(terms)
+    )(terms, scores)
 
 
 def halo_kernel(
-    wide, edge, frames, pad_one, pad_two, sides, cells, send_sem, recv_sem, own_sem
+    wide, edge, width, group, frames, cot, pad_one, pad_two, sides, spread,
+    cells, cot_wide, lanes_wide, send_sem, recv_sem, own_sem,
 ):
     row, col = lax.axis_index("row"), lax.axis_index("col")
     row_count, col_count = lax.axis_size("row"), lax.axis_size("col")
@@ -261,6 +303,17 @@
             )
             copies.append((way, copy))
             pl.when(lies(*way))(copy.start)
+    side = 2 * RAD + 1
+    chunk = group * tile_cols
+    cot_wide[...] = cot[...].astype(jnp.float32)
+    lanes_wide[...] = jnp.zeros_like(lanes_wide)
+    for block in range(spread.shape[0] // chunk):
+        at = slice(block * chunk, (block + 1) * chunk)
+        for line in range(side):
+            lanes_wide[line * width : line * width + side, :] = cot_wide[
+                line * side : (line + 1) * side, at
+            ]
+        spread[at, :] = skew(lanes_wide[...].T, tile_cols, False).astype(jnp.bfloat16)
     for copy in own:
         copy.wait()
     for way, copy in copies:
@@ -269,21 +322,24 @@
         pl.when(lies(*way))(copy.wait_send)
 
 
-def gather_halos(frames, wide, edge):
+def gather_halos(frames, cot, wide, edge, width, group, lanes):
     tile_rows, tile_cols, channels = frames.shape[1:]
     pads = [
         jax.ShapeDtypeStruct((tile_rows + 2 * halo, tile_cols + 2 * edge, channels), frames.dtype)
         for halo in (1, wide)
     ]
     pads.append(jax.ShapeDtypeStruct((2, tile_rows, channels), frames.dtype))
+    pads.append(jax.ShapeDtypeStruct((cot.shape[1], lanes), cot.dtype))
     whole = pl.BlockSpec(memory_space=pltpu.VMEM)
     return pl.pallas_call(
-        functools.partial(halo_kernel, wide, edge),
+        functools.partial(halo_kernel, wide, edge, width, group),
         out_shape=pads,
-        in_specs=[whole],
-        out_specs=[whole] * 3,
+        in_specs=[whole] * 2,
+        out_specs=[whole] * 4,
         scratch_shapes=[
             pltpu.VMEM((2, tile_rows, channels), frames.dtype),
+            pltpu.VMEM(cot.shape, jnp.float32),
+            pltpu.VMEM((lanes, group * tile_cols), jnp.float32),
             pltpu.SemaphoreType.DMA((8, 2)),
             pltpu.SemaphoreType.DMA((8, 2)),
             pltpu.SemaphoreType.DMA((2,)),
@@ -292,18 +348,19 @@
             collective_id=0, has_side_effects=True, vmem_limit_bytes=16 * 2**20
         ),
         name="gather_halos",
-    )(frames)
+    )(frames, cot)
 
 
 def tile_kernel(
-    geometry, place, pad_one, pad_two, sides, weight, bias, cot, corr, terms,
+    geometry, place, pad_one, pad_two, sides, spread_all, weight_far, bias, scores, terms,
     taps_one, taps_two, pre_one, pre_two, feat_one, feat_two, delta_one, flip_one, flip_two,
-    grad_two, cot_wide, corr_wide, lanes_wide, sides_wide,
+    grad_two, sides_wide, weight, weight_sem,
 ):
-    tile_rows, tile_cols, image_rows, image_cols, edge, width = geometry
+    tile_rows, tile_cols, image_rows, image_cols, edge, width, group = geometry
     channels = bias.shape[1]
-    side = 2 * RAD + 1
-    lanes = lanes_wide.shape[0]
+    load = pltpu.make_async_copy(weight_far, weight, weight_sem)
+    load.start()
+    lanes = spread_all.shape[1]
     padded_cols = tile_cols + 2 * edge
     window_rows = tile_rows + 2 * RAD
     pixels_two = window_rows * width
@@ -322,7 +379,7 @@
     sides_wide[:, 8 + tile_rows :, :] = jnp.zeros_like(sides_wide[:, 8 + tile_rows :, :])
     spot = across - (col_start - edge)
 
-    @pl.loop(0, tile_rows + 2)
+    @pl.loop(0, tile_rows + 2, unroll=2)
     def _(line):
         cells = pad_one[line].astype(jnp.float32)
         middle = (line > 0) & (line < tile_rows + 1)
@@ -337,7 +394,7 @@
                 cells[first : first + tile_cols].astype(jnp.bfloat16)
             )
 
-    @pl.loop(0, window_rows + 2)
+    @pl.loop(0, window_rows + 2, unroll=2)
     def _(line):
         at = shift_row + MAXOFF + line
         cells = masked(pad_two[at], row_start - (MAXOFF + RAD + 1) + at)
@@ -358,7 +415,7 @@
             )
         return total
 
-    group = 4
+    load.wait()
     size_one = group * tile_cols
 
     @pl.loop(0, tile_rows // group)
@@ -370,7 +427,7 @@
 
     size_two = group * width
 
-    @pl.loop(0, window_rows // group)
+    @pl.loop(0, window_rows // group, unroll=2)
     def _(block):
         first = pl.multiple_of(block * size_two, 16)
         pre = convolved(taps_two, first, size_two, width).reshape(group, width, channels)
@@ -385,35 +442,17 @@
 
     feat_two[pixels_two:, :] = jnp.zeros_like(feat_two[pixels_two:, :])
     grad_two[...] = jnp.zeros_like(grad_two)
-    cot_wide[...] = cot[...].astype(jnp.float32)
-    lanes_wide[...] = jnp.zeros_like(lanes_wide)
-
-    def skew(cells, back):
-        line = lax.rem(lax.broadcasted_iota(jnp.int32, cells.shape, 0), tile_cols)
-        step = 1
-        while step < tile_cols:
-            moved = pltpu.roll(cells, lanes - step if back else step, 1)
-            cells = jnp.where((line // step) % 2 == 1, moved, cells)
-            step *= 2
-        return cells
 
     @pl.loop(0, tile_rows // group)
     def _(block):
-        at = pl.ds(pl.multiple_of(block * size_one, 128), size_one)
-        for line in range(side):
-            lanes_wide[line * width : line * width + side, :] = cot_wide[
-                line * side : (line + 1) * side, at
-            ]
-        spread_all = skew(lanes_wide[...].T, False).astype(jnp.bfloat16)
-        score_list = []
         for inner in range(group):
             row = block * group + inner
-            spread = spread_all[inner * tile_cols : (inner + 1) * tile_cols]
             pixels = pl.ds(pl.multiple_of(row * tile_cols, 16), tile_cols)
             window = pl.ds(pl.multiple_of(row * width, 16), lanes)
+            spread = spread_all[pixels, :]
             one, two = feat_one[pixels, :], feat_two[window, :]
-            score_list.append(
-                lax.dot_general(one, two, (((1,), (1,)), ((), ())), preferred_element_type=jnp.float32)
+            scores[pixels, :] = lax.dot_general(
+                one, two, (((1,), (1,)), ((), ())), preferred_element_type=jnp.float32
             )
             grad = jnp.dot(spread, two, preferred_element_type=jnp.float32) * inv_root
             grad = jnp.where(pre_one[pixels, :] > 0, grad, 0.0)
@@ -421,13 +460,7 @@
             grad_two[window, :] += lax.dot_general(
                 spread, one, (((0,), (0,)), ((), ())), preferred_element_type=jnp.float32
             )
-        scores = skew(jnp.concatenate(score_list, axis=0), True).T * inv_root
-        for line in range(side):
-            corr_wide[line * side : (line + 1) * side, at] = scores[
-                line * width : line * width + side
-            ]
-
-    corr[...] = corr_wide[...].astype(jnp.bfloat16)
+
     delta_two = jnp.where(pre_two[...] > 0, grad_two[:pixels_two, :] * inv_root, 0.0)
     bias_term = jnp.sum(delta_one[...], axis=0, keepdims=True)
     bias_term = bias_term + jnp.sum(delta_two, axis=0, keepdims=True)
@@ -485,17 +518,23 @@
     long = max(pixels_two, (tile_rows - 1) * width + lanes)
     shift = offsets[0, row_start // BLK, col_start // BLK]
     place = jnp.concatenate([shift, jnp.stack([row_start, col_start])]).astype(jnp.int32)
-    pad_one, pad_two, sides = gather_halos(frames[0], wide, edge)
+    group = 4
+    cot = cotangent[0].reshape(side * side, pixels_one)
+    pad_one, pad_two, sides, spread = gather_halos(
+        frames[0], cot, wide, edge, width, group, lanes
+    )
     whole = pl.BlockSpec(memory_space=pltpu.VMEM)
     rows = padded_rows(9 * channels + 1)
-    geometry = (tile_rows, tile_cols, image_rows, image_cols, edge, width)
-    corr, terms = pl.pallas_call(
+    geometry = (tile_rows, tile_cols, image_rows, image_cols, edge, width, group)
+    scores, terms = pl.pallas_call(
         functools.partial(tile_kernel, geometry),
         out_shape=[
-            jax.ShapeDtypeStruct((side * side, pixels_one), jnp.bfloat16),
+            jax.ShapeDtypeStruct((pixels_one, lanes), jnp.float32),
             jax.ShapeDtypeStruct((2, rows, channels // 2), jnp.float32),
         ],
-        in_specs=[pl.BlockSpec(memory_space=pltpu.SMEM)] + [whole] * 6,
+        in_specs=[pl.BlockSpec(memory_space=pltpu.SMEM)]
+        + [whole] * 4
+        + [pl.BlockSpec(memory_space=pl.ANY), whole],
         out_specs=[whole] * 2,
         scratch_shapes=[
             pltpu.VMEM(((tile_rows + 2) * tile_cols, 3 * channels), jnp.bfloat16),
@@ -508,18 +547,18 @@
             pltpu.VMEM((channels, pixels_one), jnp.bfloat16),
             pltpu.VMEM((channels, pixels_two), jnp.bfloat16),
             pltpu.VMEM((long, channels), jnp.float32),
-            pltpu.VMEM((side * side, pixels_one), jnp.float32),
-            pltpu.VMEM((side * side, pixels_one), jnp.float32),
-            pltpu.VMEM((lanes, 4 * tile_cols), jnp.float32),
             pltpu.VMEM((2, tile_rows + 16, channels), jnp.float32),
+            pltpu.VMEM((3, 3 * channels, channels), jnp.bfloat16),
+            pltpu.SemaphoreType.DMA,
         ],
         compiler_params=pltpu.CompilerParams(vmem_limit_bytes=48 * 2**20),
         name="tile_terms",
     )(
-        place, pad_one, pad_two, sides, weight.reshape(3, 3 * channels, channels), bias[None],
-        cotangent[0].reshape(side * side, pixels_one),
+        place, pad_one, pad_two, sides, spread, weight.reshape(3, 3 * channels, channels),
+        bias[None],
     )
-    summed = sum_everywhere(terms)
+    shape = (tile_cols, width, group, channels ** (-0.5))
+    summed, corr = sum_everywhere(terms, scores, shape)
     grad_weight, grad_bias = pl.pallas_call(
         spread_kernel,
         out_shape=[

time: 69 us -> 65.5 us (0.949)
  Pallas kernels: 62.5 us -> 57.2 us
  local copies, waits for them, and re-layouts: 5.44 us -> 7.17 us
    pallas_call x1, Pallas kernels: 18 us -> 12.7 us  [shards(): pl.pallas_call(functools.partial(tile_kernel, geometry), out_shape=[jax.S...]
    unnamed x8 -> x10, local copies, waits for them, and re-layouts: 3.63 us -> 5.37 us
where the time goes in v4:
time: 65.5 us; the launch traced here: 65.2 us
  Pallas kernels  57.2 us (87%)
  local copies, waits for them, and re-layouts  7.17 us (11%)
  between operations  0.72 us (1%)
    pallas_call x1, Pallas kernels, sum_everywhere(): pl.pallas_call(functools.partial(sum_kernel, plans, runs, shape), out_sha...  31.4 us
    pallas_call x1, Pallas kernels, shards(): pl.pallas_call(functools.partial(tile_kernel, geometry), out_shape=[jax.S...  12.7 us
    pallas_call x1, Pallas kernels, gather_halos(): pl.pallas_call(functools.partial(halo_kernel, wide, edge, width, group),...  11.6 us
    unnamed x10, local copies, waits for them, and re-layouts  5.37 us
    pallas_call x1, Pallas kernels, shards(): pl.pallas_call(spread_kernel, out_shape=[jax.ShapeDtypeStruct((9 * channe...  1.58 us

profile of v4, /device:TPU:0, one launch (start us, length us, event | category | flops | bytes accessed | tf_op | source)
XLA Modules:
  0.0 65.2 jit_solution(1218692873087235004)
XLA Ops:
  0.6 0.0 copy-start
  0.7 0.6 copy-done
  1.3 0.1 pad_add_fusion.place
  1.4 1.0 %copy.10.cot = bf16[81,512]{1,0:T(8,128)(2,1)S(1)} copy(bf16[81,512]{0,1:T(8,128)(2,1)} %bitcast.14) | data formatting | bytes 165888 | tf_op jit(solution)/shard_map/reshape;squeeze | solution.py:522
  2.4 0.0 copy-start.3
  2.4 1.0 %copy-done.3 = bf16[1,2,16,32,256]{4,3,2,1,0:T(8,128)(2,1)S(1)} copy-done((bf16[1,2,16,32,256]{4,3,2,1,0:T(8,128)(2,1)S(1)}, bf16[1,2,16,32,256]{4,3,2,1,0:T(8,128)(2,1)}, u32[]{:S(2)}) %copy-start.3) | copy-done | bytes 524312
  3.5 11.6 %gather_halos.1 = (bf16[18,64,256]{2,1,0:T(8,128)(2,1)S(1)}, bf16[42,64,256]{2,1,0:T(8,128)(2,1)S(1)}, bf16[2,16,256]{2,1,0:T(8,128)(2,1)S(1)}, bf16[512,512]{1,0:T(8,128)(2,1)S(1)}) custom-call(bf16[2,16,32,256]{3,2,1,0:T(8,128)(2,1)S(1)} %bitcast.12, bf16[81,512]{1,0:T(8,128)(2,1)S(1)} %copy.10.cot), custom_call_target="tpu_custom_call" | custom-call | tf_op jit(solution)/shard_map/gather_halos/pallas_call | solution.py:334
  15.1 0.0 copy-start.2
  15.1 1.3 %copy-done.2 = bf16[3,3,256,256]{3,2,1,0:T(8,128)(2,1)S(1)} copy-done((bf16[3,3,256,256]{3,2,1,0:T(8,128)(2,1)S(1)}, bf16[3,3,256,256]{3,2,1,0:T(8,128)(2,1)}, u32[]{:S(2)}) %copy-start.2) | copy-done | bytes 1179672
  16.3 0.0 copy-start.4
  16.3 0.7 %copy-done.4 = f32[256]{0:T(256)S(1)} copy-done((f32[256]{0:T(256)S(1)}, f32[256]{0:T(256)}, u32[]{:S(2)}) %copy-start.4) | copy-done | bytes 1048
  17.0 12.7 %tile_terms.1 = (f32[512,512]{1,0:T(8,128)S(1)}, f32[2,2560,128]{2,1,0:T(8,128)}) custom-call(s32[4]{0:T(128)S(1)} %pad_add_fusion.place, bf16[18,64,256]{2,1,0:T(8,128)(2,1)S(1)} %get-tuple-element.13.pad_one, bf16[42,64,256]{2,1,0:T(8,128)(2,1)S(1)} %get-tuple-element.14.pad_two, bf16[2,16,256]{2,1,0:T(8,128)(2,1)S(1)} %get-tuple-element.15.sides, ...), custom_call_target="tpu_custom_call" | custom-call | tf_op jit(solution)/shard_map/tile_terms/pallas_call | solution.py:529
  29.7 0.0 copy-start.1
  29.7 1.7 %copy-done.1 = f32[2,2560,128]{2,1,0:T(8,128)S(1)} copy-done((f32[2,2560,128]{2,1,0:T(8,128)S(1)}, f32[2,2560,128]{2,1,0:T(8,128)}, u32[]{:S(2)}) %copy-start.1) | copy-done | bytes 2621464
  31.5 31.4 %sum_everywhere.1 = (bf16[2,2560,128]{2,1,0:T(8,128)(2,1)S(1)}, bf16[81,512]{1,0:T(8,128)(2,1)S(1)}) custom-call(f32[2,2560,128]{2,1,0:T(8,128)S(1)} %copy-done.1, f32[512,512]{1,0:T(8,128)S(1)} %get-tuple-element.18.scores), custom_call_target="tpu_custom_call" | custom-call | tf_op jit(solution)/shard_map/sum_everywhere/pallas_call | solution.py:217
  62.8 0.8 %copy.11 = bf16[81,512]{0,1:T(8,128)(2,1)} copy(bf16[81,512]{1,0:T(8,128)(2,1)S(1)} %get-tuple-element.19) | data formatting | bytes 165888 | tf_op jit(solution)/shard_map/sum_everywhere/pallas_call | solution.py:217
  63.6 1.6 %spread_sum.1 = (f32[2304,256]{1,0:T(8,128)}, f32[1,256]{1,0:T(1,128)}) custom-call(bf16[2,2560,128]{2,1,0:T(8,128)(2,1)S(1)} %get-tuple-element.20.summed), custom_call_target="tpu_custom_call" | custom-call | tf_op jit(solution)/shard_map/spread_sum/pallas_call | solution.py:562
  (1 shorter events, 0.0 us)
Async XLA Ops:
  0.6 0.7 %copy-start = (s32[1,2,2,2]{3,2,1,0:T(2,128)S(1)}, s32[1,2,2,2]{3,2,1,0:T(2,128)}, u32[]{:S(2)}) copy-start(s32[1,2,2,2]{3,2,1,0:T(2,128)} %param.6) | copy-start | bytes 100
  2.4 1.0 %copy-start.3 = (bf16[1,2,16,32,256]{4,3,2,1,0:T(8,128)(2,1)S(1)}, bf16[1,2,16,32,256]{4,3,2,1,0:T(8,128)(2,1)}, u32[]{:S(2)}) copy-start(bf16[1,2,16,32,256]{4,3,2,1,0:T(8,128)(2,1)} %param.5) | copy-start | bytes 1572868
  15.1 1.3 %copy-start.2 = (bf16[3,3,256,256]{3,2,1,0:T(8,128)(2,1)S(1)}, bf16[3,3,256,256]{3,2,1,0:T(8,128)(2,1)}, u32[]{:S(2)}) copy-start(bf16[3,3,256,256]{3,2,1,0:T(8,128)(2,1)} %param.7) | copy-start | bytes 3538948
  16.3 0.7 %copy-start.4 = (f32[256]{0:T(256)S(1)}, f32[256]{0:T(256)}, u32[]{:S(2)}) copy-start(f32[256]{0:T(256)} %param.8) | copy-start | bytes 3076
  29.7 1.7 %copy-start.1 = (f32[2,2560,128]{2,1,0:T(8,128)S(1)}, f32[2,2560,128]{2,1,0:T(8,128)}, u32[]{:S(2)}) copy-start(f32[2,2560,128]{2,1,0:T(8,128)} %get-tuple-element.17.terms) | copy-start | bytes 7864324

commit v5 on v4

--- a/solution.py
+++ b/solution.py
@@ -22,6 +22,19 @@
         cells = jnp.where((line // step) % 2 == 1, moved, cells)
         step *= 2
     return cells
+
+
+def band_places(width, lanes):
+    side = 2 * RAD + 1
+    shape = (side * side, lanes)
+    band = lax.broadcasted_iota(jnp.int32, shape, 0)
+    lane = lax.broadcasted_iota(jnp.int32, shape, 1)
+    found = jnp.zeros(shape, jnp.float32)
+    for line in range(side):
+        first = line * width
+        here = (lane - band == line * (width - side)) & (lane >= first) & (lane < first + side)
+        found = jnp.where(here, 1.0, found)
+    return found
 
 
 def exchange_plan():
@@ -38,7 +51,7 @@
 
 def sum_kernel(
     plans, runs, shape, terms, scores, total, corr,
-    acc, send_half, recv_half, recv_wide, corr_wide, *sems,
+    acc, send_half, recv_half, recv_wide, *sems,
 ):
     rs_send, rs_recv, ag_send, ag_recv, far_send, far_recv = sems
     count = len(plans[0])
@@ -63,22 +76,19 @@
     pl.semaphore_wait(barrier, count + depth - 1)
 
     tile_cols, width, group, inv_root = shape
-    side = 2 * RAD + 1
     chunk = group * tile_cols
+    places = band_places(width, scores.shape[1]).astype(jnp.bfloat16)
     blocks = list(range(scores.shape[0] // chunk))
 
     def take_band():
         if not blocks:
             return
         at = slice(blocks[0] * chunk, (blocks[0] + 1) * chunk)
-        bands = skew(scores[at, :], tile_cols, True).T * inv_root
-        for line in range(side):
-            corr_wide[line * side : (line + 1) * side, at] = bands[
-                line * width : line * width + side
-            ]
+        bands = (skew(scores[at, :], tile_cols, True) * inv_root).astype(jnp.bfloat16)
+        corr[at, :] = lax.dot_general(
+            bands, places, (((1,), (1,)), ((), ())), preferred_element_type=jnp.float32
+        ).astype(jnp.bfloat16)
         blocks.pop(0)
-        if not blocks:
-            corr[...] = corr_wide[...].astype(jnp.bfloat16)
 
     base = [start for _, start, _ in runs]
     trail = [[] for _ in parts]
@@ -218,7 +228,7 @@
         functools.partial(sum_kernel, plans, runs, shape),
         out_shape=[
             jax.ShapeDtypeStruct(terms.shape, jnp.bfloat16),
-            jax.ShapeDtypeStruct(((2 * RAD + 1) ** 2, scores.shape[0]), jnp.bfloat16),
+            jax.ShapeDtypeStruct((scores.shape[0], (2 * RAD + 1) ** 2), jnp.bfloat16),
         ],
         in_specs=[pl.BlockSpec(memory_space=pltpu.VMEM)] * 2,
         out_specs=[pl.BlockSpec(memory_space=pltpu.VMEM)] * 2,
@@ -227,7 +237,6 @@
             pltpu.VMEM(terms.shape, jnp.bfloat16),
             pltpu.VMEM(terms.shape, jnp.bfloat16),
             pltpu.VMEM(terms.shape, jnp.float32),
-            pltpu.VMEM(((2 * RAD + 1) ** 2, scores.shape[0]), jnp.float32),
             near,
             near,
             near,
@@ -236,7 +245,7 @@
             far,
         ],
         compiler_params=pltpu.CompilerParams(
-            collective_id=1, has_side_effects=True, vmem_limit_bytes=32 * 2**20
+            collective_id=1, has_side_effects=True, vmem_limit_bytes=20 * 2**20
         ),
         name="sum_everywhere",
     )(terms, scores)
@@ -244,7 +253,7 @@
 
 def halo_kernel(
     wide, edge, width, group, frames, cot, pad_one, pad_two, sides, spread,
-    cells, cot_wide, lanes_wide, send_sem, recv_sem, own_sem,
+    cells, send_sem, recv_sem, own_sem,
 ):
     row, col = lax.axis_index("row"), lax.axis_index("col")
     row_count, col_count = lax.axis_size("row"), lax.axis_size("col")
@@ -303,17 +312,12 @@
             )
             copies.append((way, copy))
             pl.when(lies(*way))(copy.start)
-    side = 2 * RAD + 1
     chunk = group * tile_cols
-    cot_wide[...] = cot[...].astype(jnp.float32)
-    lanes_wide[...] = jnp.zeros_like(lanes_wide)
+    places = band_places(width, spread.shape[1]).astype(jnp.bfloat16)
     for block in range(spread.shape[0] // chunk):
         at = slice(block * chunk, (block + 1) * chunk)
-        for line in range(side):
-            lanes_wide[line * width : line * width + side, :] = cot_wide[
-                line * side : (line + 1) * side, at
-            ]
-        spread[at, :] = skew(lanes_wide[...].T, tile_cols, False).astype(jnp.bfloat16)
+        bands = jnp.dot(cot[at, :], places, preferred_element_type=jnp.float32)
+        spread[at, :] = skew(bands, tile_cols, False).astype(jnp.bfloat16)
     for copy in own:
         copy.wait()
     for way, copy in copies:
@@ -329,7 +333,7 @@
         for halo in (1, wide)
     ]
     pads.append(jax.ShapeDtypeStruct((2, tile_rows, channels), frames.dtype))
-    pads.append(jax.ShapeDtypeStruct((cot.shape[1], lanes), cot.dtype))
+    pads.append(jax.ShapeDtypeStruct((cot.shape[0], lanes), cot.dtype))
     whole = pl.BlockSpec(memory_space=pltpu.VMEM)
     return pl.pallas_call(
         functools.partial(halo_kernel, wide, edge, width, group),
@@ -338,8 +342,6 @@
         out_specs=[whole] * 4,
         scratch_shapes=[
             pltpu.VMEM((2, tile_rows, channels), frames.dtype),
-            pltpu.VMEM(cot.shape, jnp.float32),
-            pltpu.VMEM((lanes, group * tile_cols), jnp.float32),
             pltpu.SemaphoreType.DMA((8, 2)),
             pltpu.SemaphoreType.DMA((8, 2)),
             pltpu.SemaphoreType.DMA((2,)),
@@ -519,7 +521,7 @@
     shift = offsets[0, row_start // BLK, col_start // BLK]
     place = jnp.concatenate([shift, jnp.stack([row_start, col_start])]).astype(jnp.int32)
     group = 4
-    cot = cotangent[0].reshape(side * side, pixels_one)
+    cot = jnp.transpose(cotangent[0], (1, 2, 0)).reshape(pixels_one, side * side)
     pad_one, pad_two, sides, spread = gather_halos(
         frames[0], cot, wide, edge, width, group, lanes
     )
@@ -551,7 +553,7 @@
             pltpu.VMEM((3, 3 * channels, channels), jnp.bfloat16),
             pltpu.SemaphoreType.DMA,
         ],
-        compiler_params=pltpu.CompilerParams(vmem_limit_bytes=48 * 2**20),
+        compiler_params=pltpu.CompilerParams(vmem_limit_bytes=24 * 2**20),
         name="tile_terms",
     )(
         place, pad_one, pad_two, sides, spread, weight.reshape(3, 3 * channels, channels),
@@ -567,11 +569,11 @@
         ],
         in_specs=[whole],
         out_specs=[whole] * 2,
-        compiler_params=pltpu.CompilerParams(vmem_limit_bytes=32 * 2**20),
+        compiler_params=pltpu.CompilerParams(vmem_limit_bytes=12 * 2**20),
         name="spread_sum",
     )(summed)
     return (
-        corr.reshape(1, side * side, tile_rows, tile_cols),
+        jnp.transpose(corr.reshape(tile_rows, tile_cols, side * side), (2, 0, 1))[None],
         grad_weight.reshape(weight.shape),
         grad_bias[0],
     )

time: 65.5 us -> 62 us (0.947)
  local copies, waits for them, and re-layouts: 7.17 us -> 5.19 us
  Pallas kernels: 57.2 us -> 55.8 us
    pallas_call x1, Pallas kernels: 12.7 us -> 11.2 us  [shards(): pl.pallas_call(functools.partial(tile_kernel, geometry), out_shape=[jax.S...]
    another operation x1 -> x0, local copies, waits for them, and re-layouts: 1.02 us -> none  [shards(): cot = cotangent[0].reshape(side * side, pixels_one)]
    pallas_call x1 -> x0, local copies, waits for them, and re-layouts: 0.77 us -> none  [sum_everywhere(): pl.pallas_call(functools.partial(sum_kernel, plans, runs, shape), out_sha...]
    unnamed x10 -> x11, local copies, waits for them, and re-layouts: 5.37 us -> 5.19 us
where the time goes in v5:
time: 62 us; the launch traced here: 61.8 us
  Pallas kernels  55.8 us (90%)
  local copies, waits for them, and re-layouts  5.19 us (8%)
  between operations  0.71 us (1%)
    pallas_call x1, Pallas kernels, sum_everywhere(): pl.pallas_call(functools.partial(sum_kernel, plans, runs, shape), out_sha...  31.4 us
    pallas_call x1, Pallas kernels, gather_halos(): pl.pallas_call(functools.partial(halo_kernel, wide, edge, width, group),...  11.6 us
    pallas_call x1, Pallas kernels, shards(): pl.pallas_call(functools.partial(tile_kernel, geometry), out_shape=[jax.S...  11.2 us
    unnamed x11, local copies, waits for them, and re-layouts  5.19 us
    pallas_call x1, Pallas kernels, shards(): pl.pallas_call(spread_kernel, out_shape=[jax.ShapeDtypeStruct((9 * channe...  1.58 us

profile of v5, /device:TPU:0, one launch (start us, length us, event | category | flops | bytes accessed | tf_op | source)
XLA Modules:
  0.0 61.8 jit_solution(10499729468026052869)
XLA Ops:
  0.6 0.0 copy-start
  0.7 0.6 %copy-done = s32[1,2,2,2]{3,2,1,0:T(2,128)S(1)} copy-done((s32[1,2,2,2]{3,2,1,0:T(2,128)S(1)}, s32[1,2,2,2]{3,2,1,0:T(2,128)}, u32[]{:S(2)}) %copy-start) | copy-done | bytes 56
  1.3 0.1 pad_add_fusion.place
  1.4 0.0 copy-start.2
  1.4 1.0 %copy-done.2 = bf16[1,2,16,32,256]{4,3,2,1,0:T(8,128)(2,1)S(1)} copy-done((bf16[1,2,16,32,256]{4,3,2,1,0:T(8,128)(2,1)S(1)}, bf16[1,2,16,32,256]{4,3,2,1,0:T(8,128)(2,1)}, u32[]{:S(2)}) %copy-start.2) | copy-done | bytes 524312
  2.4 0.0 copy-start.3
  2.4 0.9 %copy-done.3 = bf16[1,81,16,32]{1,3,2,0:T(8,128)(2,1)S(1)} copy-done((bf16[1,81,16,32]{1,3,2,0:T(8,128)(2,1)S(1)}, bf16[1,81,16,32]{1,3,2,0:T(8,128)(2,1)}, u32[]{:S(2)}) %copy-start.3) | copy-done | bytes 82968
  3.4 11.6 %gather_halos.1 = (bf16[18,64,256]{2,1,0:T(8,128)(2,1)S(1)}, bf16[42,64,256]{2,1,0:T(8,128)(2,1)S(1)}, bf16[2,16,256]{2,1,0:T(8,128)(2,1)S(1)}, bf16[512,512]{1,0:T(8,128)(2,1)S(1)}) custom-call(bf16[2,16,32,256]{3,2,1,0:T(8,128)(2,1)S(1)} %bitcast.20, bf16[512,81]{1,0:T(8,128)(2,1)S(1)} %bitcast.21), custom_call_target="tpu_custom_call" | custom-call | tf_op jit(solution)/shard_map/gather_halos/pallas_call | solution.py:338
  14.9 0.0 copy-start.1
  14.9 1.3 %copy-done.1 = bf16[3,3,256,256]{3,2,1,0:T(8,128)(2,1)S(1)} copy-done((bf16[3,3,256,256]{3,2,1,0:T(8,128)(2,1)S(1)}, bf16[3,3,256,256]{3,2,1,0:T(8,128)(2,1)}, u32[]{:S(2)}) %copy-start.1) | copy-done | bytes 1179672
  16.2 0.0 copy-start.4
  16.2 0.7 %copy-done.4 = f32[256]{0:T(256)S(1)} copy-done((f32[256]{0:T(256)S(1)}, f32[256]{0:T(256)}, u32[]{:S(2)}) %copy-start.4) | copy-done | bytes 1048
  16.9 11.2 %tile_terms.1 = (f32[512,512]{1,0:T(8,128)S(1)}, f32[2,2560,128]{2,1,0:T(8,128)S(1)}) custom-call(s32[4]{0:T(128)S(1)} %pad_add_fusion.place, bf16[18,64,256]{2,1,0:T(8,128)(2,1)S(1)} %get-tuple-element.13.pad_one, bf16[42,64,256]{2,1,0:T(8,128)(2,1)S(1)} %get-tuple-element.14.pad_two, bf16[2,16,256]{2,1,0:T(8,128)(2,1)S(1)} %get-tuple-element.15.sides, ...), custom_call_target="tpu_custom_call" | custom-call | tf_op jit(solution)/shard_map/tile_terms/pallas_call | solution.py:531
  28.1 31.4 %sum_everywhere.1 = (bf16[2,2560,128]{2,1,0:T(8,128)(2,1)S(1)}, bf16[512,81]{1,0:T(8,128)(2,1)S(1)}) custom-call(f32[2,2560,128]{2,1,0:T(8,128)S(1)} %get-tuple-element.17.terms, f32[512,512]{1,0:T(8,128)S(1)} %get-tuple-element.18.scores), custom_call_target="tpu_custom_call" | custom-call | tf_op jit(solution)/shard_map/sum_everywhere/pallas_call | solution.py:227
  59.6 1.6 %spread_sum.1 = (f32[2304,256]{1,0:T(8,128)}, f32[1,256]{1,0:T(1,128)}) custom-call(bf16[2,2560,128]{2,1,0:T(8,128)(2,1)S(1)} %get-tuple-element.20.summed), custom_call_target="tpu_custom_call" | custom-call | tf_op jit(solution)/shard_map/spread_sum/pallas_call | solution.py:564
  61.1 0.7 %copy.9 = bf16[1,81,16,32]{1,3,2,0:T(8,128)(2,1)} copy(bf16[1,81,16,32]{1,3,2,0:T(8,128)(2,1)S(1)} %bitcast.22) | data formatting | bytes 165888
  (1 shorter events, 0.0 us)
Async XLA Ops:
  0.6 0.7 %copy-start = (s32[1,2,2,2]{3,2,1,0:T(2,128)S(1)}, s32[1,2,2,2]{3,2,1,0:T(2,128)}, u32[]{:S(2)}) copy-start(s32[1,2,2,2]{3,2,1,0:T(2,128)} %param.6) | copy-start | bytes 100
  1.4 1.0 %copy-start.2 = (bf16[1,2,16,32,256]{4,3,2,1,0:T(8,128)(2,1)S(1)}, bf16[1,2,16,32,256]{4,3,2,1,0:T(8,128)(2,1)}, u32[]{:S(2)}) copy-start(bf16[1,2,16,32,256]{4,3,2,1,0:T(8,128)(2,1)} %param.5) | copy-start | bytes 1572868
  2.4 0.9 %copy-start.3 = (bf16[1,81,16,32]{1,3,2,0:T(8,128)(2,1)S(1)}, bf16[1,81,16,32]{1,3,2,0:T(8,128)(2,1)}, u32[]{:S(2)}) copy-start(bf16[1,81,16,32]{1,3,2,0:T(8,128)(2,1)} %param.9) | copy-start | bytes 248836
  14.9 1.3 %copy-start.1 = (bf16[3,3,256,256]{3,2,1,0:T(8,128)(2,1)S(1)}, bf16[3,3,256,256]{3,2,1,0:T(8,128)(2,1)}, u32[]{:S(2)}) copy-start(bf16[3,3,256,256]{3,2,1,0:T(8,128)(2,1)} %param.7) | copy-start | bytes 3538948
  16.2 0.7 %copy-start.4 = (f32[256]{0:T(256)S(1)}, f32[256]{0:T(256)}, u32[]{:S(2)}) copy-start(f32[256]{0:T(256)} %param.8) | copy-start | bytes 3076
